TPU v7x, 256 devices: a whole 4x4x8 slice. The times are simulated.
256 devices in a mesh: leaf: 64 (over y, z, core), row: 4 (over x).
Axes of the slice: x: 4, y: 4, z: 8, core: 2. Of those that a mesh axis runs over, the one named last changes fastest.
Arguments:
- fields: bfloat16 [256, 2048, 128], P('leaf', 'row'), may hold values from -6 to 6
- near_blocks: bfloat16 [256, 2048, 2048], P('leaf', 'row'), may hold values from -1 to 1, as said below
- leaf_basis: bfloat16 [256, 2048, 256], P('leaf', 'row'), may hold values from -0.125 to 0.125
- leaf_transfer: bfloat16 [256, 256, 256], P('leaf'), may hold values from -0.3125 to 0.3125
- mid_transfer: bfloat16 [128, 256, 256], P('leaf'), may hold values from -0.3125 to 0.3125
- leaf_couple: bfloat16 [128, 256, 256], P('leaf'), may hold values from -0.375 to 0.375
- mid_couple: bfloat16 [64, 256, 256], P('leaf'), may hold values from -0.375 to 0.375
- cross_transfer: bfloat16 [64, 5, 256, 256], P('leaf'), may hold values from -1 to 1, as said below
- cross_couple: bfloat16 [64, 6, 256, 256], P('leaf'), may hold values from -1 to 1, as said below
Outputs:
- product: bfloat16 [256, 2048, 128], P('leaf', 'row')
Inputs may be any that keep to these rules, and one draw needn't show every extreme that they name: Each near_blocks[n] is symmetric. cross_transfer[d, j] is equal for all d with the same d >> j: the transfer matrix of node d >> j at height j + 2. cross_couple[d, j] is equal for all d with the same d >> j, and for siblings it is the transpose of the other's.
All inputs are finite; a program needn't handle non-finite values.
Results may differ from a plain program's by a relative error of at most 0.0038.
Values may be sent and summed in bfloat16 or wider, within the bound.
No kernel may reach another device: no remote copies, remote signals or barrier semaphores. Data moves between devices by JAX's collectives and lax.ppermute only.
A program may use at most 64 MiB of HBM per device.

v0:
```python
import jax
import jax.numpy as jnp
from jax import lax
from jax.sharding import PartitionSpec as P

precise = lax.Precision.HIGHEST


def swapped(block, axis, bit):
    count = lax.axis_size(axis)
    route = []
    for low in range(count):
        high = low | 1 << bit
        if high != low and high < count:
            route += [(low, high), (high, low)]
    return lax.ppermute(block, axis, route)


def lift(mats, skel):
    return jnp.einsum("nrs,nrc->nsc", mats.astype(jnp.float32), skel, precision=precise)


def push(mats, potential):
    return jnp.einsum("nrs,nsc->nrc", mats.astype(jnp.float32), potential, precision=precise)


def pair_sums(values):
    return values.reshape((-1, 2) + values.shape[1:]).sum(axis=1)


def couple_pairs(mats, skel):
    mats32 = mats.astype(jnp.float32)
    left_skel = skel[0::2]
    right_skel = skel[1::2]
    to_left = jnp.einsum("prs,psc->prc", mats32, right_skel, precision=precise)
    to_right = jnp.einsum("psr,psc->prc", mats32, left_skel, precision=precise)
    return jnp.stack([to_left, to_right], axis=1).reshape(skel.shape)


def shards(
    fields,
    near_blocks,
    leaf_basis,
    leaf_transfer,
    mid_transfer,
    leaf_couple,
    mid_couple,
    cross_transfer,
    cross_couple,
):
    levels_above = lax.axis_size("leaf").bit_length() - 1
    partial_skel = jnp.einsum(
        "nkr,nkc->nrc", leaf_basis, fields, preferred_element_type=jnp.float32
    )
    skel_leaf = lax.psum(partial_skel, "row")
    skel_mid = pair_sums(lift(leaf_transfer, skel_leaf))
    current = pair_sums(lift(mid_transfer, skel_mid))[0]
    lift_mats = cross_transfer[0].astype(jnp.float32)
    couple_mats = cross_couple[0].astype(jnp.float32)
    received = []
    for height in range(levels_above - 1):
        outgoing = jnp.dot(couple_mats[height].T, current, precision=precise)
        lifted = jnp.dot(lift_mats[height].T, current, precision=precise)
        incoming, partner = swapped((outgoing, lifted), "leaf", height)
        received.append(incoming)
        current = lifted + partner
    crown = levels_above - 1
    potential = swapped(jnp.dot(couple_mats[crown].T, current, precision=precise), "leaf", crown)
    for height in reversed(range(levels_above - 1)):
        potential = jnp.dot(lift_mats[height], potential, precision=precise) + received[height]
    pot_mid = push(mid_transfer, jnp.repeat(potential[None], 2, axis=0)) + couple_pairs(
        mid_couple, skel_mid
    )
    pot_leaf = push(leaf_transfer, jnp.repeat(pot_mid, 2, axis=0)) + couple_pairs(
        leaf_couple, skel_leaf
    )
    potential_low = pot_leaf.astype(jnp.bfloat16)
    far_part = jnp.einsum(
        "nkr,nrc->nkc", leaf_basis, potential_low, preferred_element_type=jnp.float32
    )
    near_part = jnp.einsum(
        "nrk,nkc->nrc",
        near_blocks,
        lax.all_gather(fields, "row", axis=1, tiled=True),
        preferred_element_type=jnp.float32,
    )
    return (near_part + far_part).astype(jnp.bfloat16)


def solution(mesh):
    return jax.shard_map(
        shards,
        mesh=mesh,
        in_specs=(
            P("leaf", "row", None),
            P("leaf", "row", None),
            P("leaf", "row", None),
            P("leaf", None, None),
            P("leaf", None, None),
            P("leaf", None, None),
            P("leaf", None, None),
            P("leaf", None, None, None),
            P("leaf", None, None, None),
        ),
        out_specs=P("leaf", "row", None),
        check_vma=False,
    )
```

profile of v0, /device:TPU:4, one launch (start us, length us, event | category | flops | bytes accessed | tf_op | source)
XLA Modules:
  0.0 142.3 jit_solution(2052152148627785598)
XLA Ops:
  6.5 0.0 copy-start
  6.5 0.0 all-reduce.2.cloned.1.call-start
  6.5 1.2 copy-done
  7.8 2.4 %fusion.57 = f32[4,256,128]{2,1,0:T(8,128)} fusion(bf16[4,512,256]{2,1,0:T(8,128)(2,1)S(1)} %copy-done, bf16[4,512,128]{2,1,0:T(8,128)(2,1)} %param.9), kind=kOutput, calls=%fused_computation.86 | convolution fusion | flops 134217728 | bytes 2097152 | tf_op jit(solution)/shard_map/nkr,nkc->nrc/dot_general | solution.py:52
  10.1 0.0 all-reduce.2.cloned.1.call-update
  10.1 0.0 all-gather.2.cloned.1.call-start
  10.2 0.7 all-gather.2.cloned.1.call-update
  10.9 0.0 copy-start.2
  10.9 49.8 %all-reduce.2.cloned.1.call-done = f32[4,256,128]{2,1,0:T(8,128)} async-done(((f32[4,256,128]{2,1,0:T(8,128)}), f32[4,256,128]{2,1,0:T(8,128)}) %all-reduce.2.cloned.1.call-update) | async-done | bytes 524304 | tf_op jit(solution)/shard_map/psum | solution.py:55
  60.7 1.9 %bitcast_reduce_fusion = f32[2,256,128]{1,2,0:T(8,128)S(1)} fusion(f32[4,256,128]{2,1,0:T(8,128)} %all-reduce.2.cloned.1.call-done, bf16[4,256,256]{2,1,0:T(8,128)(2,1)} %param.12), kind=kOutput, calls=%fused_computation.33 | convolution fusion | flops 402718720 | bytes 1310720 | tf_op jit(solution)/shard_map/nrs,nrc->nsc/dot_general | solution.py:20
  62.6 1.2 convolution_bitcast_fusion.5
  63.8 1.1 convolution_bitcast_fusion.23
  65.0 0.0 copy-start.3
  65.0 1.8 %convolution_bitcast_fusion.8 = f32[256,128]{0,1:T(8,128)} fusion(f32[128,256]{1,0:T(8,128)S(1)} %convolution_bitcast_fusion.5, bf16[1,6,256,256]{3,2,1,0:T(8,128)(2,1)} %param.17), kind=kOutput, calls=%fused_computation.13 | convolution fusion | flops 100663296 | bytes 393216 | tf_op jit(solution)/shard_map/dot_general | solution.py:62
  66.8 1.8 %convolution_bitcast_fusion.6 = f32[1,1,256,128]{2,3,1,0:T(8,128)} fusion(f32[2,256,128]{1,2,0:T(8,128)S(1)} %bitcast_reduce_fusion, bf16[1,256,256]{2,1,0:T(8,128)(2,1)} %param.15), kind=kOutput, calls=%fused_computation.11 | convolution fusion | flops 100663296 | bytes 393216 | tf_op jit(solution)/shard_map/psr,psc->prc/dot_general | solution.py:36
  68.6 0.0 collective-permute-start.10
  68.6 0.5 collective-permute-start
  69.1 1.5 %convolution_bitcast_fusion.2 = f32[2,1,256,128]{2,3,0,1:T(8,128)S(1)} fusion(bf16[2,256,256]{2,1,0:T(8,128)(2,1)} %param.14, f32[4,256,128]{2,1,0:T(8,128)} %all-reduce.2.cloned.1.call-done), kind=kOutput, calls=%fused_computation.6 | convolution fusion | flops 201326592 | bytes 786432 | tf_op jit(solution)/shard_map/psr,psc->prc/dot_general | solution.py:36
  70.6 1.5 %convolution_bitcast_fusion.3 = f32[2,1,256,128]{2,3,0,1:T(8,128)S(1)} fusion(bf16[2,256,256]{2,1,0:T(8,128)(2,1)} %param.14, f32[4,256,128]{2,1,0:T(8,128)} %all-reduce.2.cloned.1.call-done), kind=kOutput, calls=%fused_computation.7 | convolution fusion | flops 201326592 | bytes 786432 | tf_op jit(solution)/shard_map/prs,psc->prc/dot_general | solution.py:35
  72.0 0.0 collective-permute-done
  72.1 0.0 copy-start.4
  72.1 1.8 %convolution_bitcast_fusion.22 = f32[256,128]{0,1:T(8,128)} fusion(bf16[1,5,256,256]{3,2,1,0:T(8,128)(2,1)} %param.16, f32[256,128]{0,1:T(8,128)S(1)} %convolution_bitcast_fusion.23, f32[256,128]{0,1:T(8,128)S(1)} %collective-permute-done), kind=kOutput, calls=%fused_computation.27 | convolution fusion | flops 100696064 | bytes 524288 | tf_op jit(solution)/shard_map/dot_general | solution.py:63
  73.9 1.6 %collective-permute-start.1 = (f32[256,128]{0,1:T(8,128)}, f32[256,128]{0,1:T(8,128)}, u32[]{:S(2)}, u32[]{:S(2)}) collective-permute-start(f32[256,128]{0,1:T(8,128)} %convolution_bitcast_fusion.22), channel_id=1, source_target_pairs={{0,8},{8,0},{4,12},{12,4},{16,24},{24,16},{20,28},{28,20},{32,40},... | collective-permute-start | bytes 393224 | tf_op jit(solution)/shard_map/ppermute | solution.py:16
  75.5 0.0 copy-done.3
  75.5 0.0 copy-done.4
  75.5 0.2 copy.21
  75.7 1.2 convolution_bitcast_fusion.7
  76.9 2.7 %collective-permute-done.1 = f32[256,128]{0,1:T(8,128)} collective-permute-done((f32[256,128]{0,1:T(8,128)}, f32[256,128]{0,1:T(8,128)}, u32[]{:S(2)}, u32[]{:S(2)}) %collective-permute-start.1) | collective-permute-done | bytes 131104 | tf_op jit(solution)/shard_map/ppermute | solution.py:16
  79.6 1.2 convolution_bitcast_fusion.21
  80.8 2.6 %collective-permute-start.2 = (f32[256,128]{0,1:T(8,128)S(1)}, f32[256,128]{0,1:T(8,128)S(1)}, u32[]{:S(2)}, u32[]{:S(2)}) collective-permute-start(f32[256,128]{0,1:T(8,128)S(1)} %convolution_bitcast_fusion.21), channel_id=1, source_target_pairs={{0,16},{16,0},{4,20},{20,4},{8,24},{24,8},{12,28},{28,12},{32,48},... | collective-permute-start | bytes 393224 | tf_op jit(solution)/shard_map/ppermute | solution.py:16
  83.5 1.3 convolution_bitcast_fusion.10
  84.7 1.6 %collective-permute-start.9 = (f32[256,128]{0,1:T(8,128)S(1)}, f32[256,128]{0,1:T(8,128)S(1)}, u32[]{:S(2)}, u32[]{:S(2)}) collective-permute-start(f32[256,128]{0,1:T(8,128)S(1)} %convolution_bitcast_fusion.10), channel_id=1, source_target_pairs={{0,8},{8,0},{4,12},{12,4},{16,24},{24,16},{20,28},{28,20},{32,40},... | collective-permute-start | bytes 393224 | tf_op jit(solution)/shard_map/ppermute | solution.py:16
  86.4 2.8 %collective-permute-done.2 = f32[256,128]{0,1:T(8,128)S(1)} collective-permute-done((f32[256,128]{0,1:T(8,128)S(1)}, f32[256,128]{0,1:T(8,128)S(1)}, u32[]{:S(2)}, u32[]{:S(2)}) %collective-permute-start.2) | collective-permute-done | bytes 131104 | tf_op jit(solution)/shard_map/ppermute | solution.py:16
  89.2 0.2 convolution_bitcast_fusion.20
  89.5 5.8 %collective-permute-start.3 = (f32[256,128]{0,1:T(8,128)S(1)}, f32[256,128]{0,1:T(8,128)S(1)}, u32[]{:S(2)}, u32[]{:S(2)}) collective-permute-start(f32[256,128]{0,1:T(8,128)S(1)} %convolution_bitcast_fusion.20), channel_id=1, source_target_pairs={{0,32},{32,0},{4,36},{36,4},{8,40},{40,8},{12,44},{44,12},{16,48},... | collective-permute-start | bytes 393224 | tf_op jit(solution)/shard_map/ppermute | solution.py:16
  95.3 1.3 convolution_bitcast_fusion.12
  96.6 0.1 collective-permute-start.8
  96.7 6.1 %collective-permute-done.3 = f32[256,128]{0,1:T(8,128)S(1)} collective-permute-done((f32[256,128]{0,1:T(8,128)S(1)}, f32[256,128]{0,1:T(8,128)S(1)}, u32[]{:S(2)}, u32[]{:S(2)}) %collective-permute-start.3) | collective-permute-done | bytes 131104 | tf_op jit(solution)/shard_map/ppermute | solution.py:16
  102.8 0.2 convolution_bitcast_fusion.19
  103.0 1.6 %collective-permute-start.4 = (f32[256,128]{0,1:T(8,128)S(1)}, f32[256,128]{0,1:T(8,128)S(1)}, u32[]{:S(2)}, u32[]{:S(2)}) collective-permute-start(f32[256,128]{0,1:T(8,128)S(1)} %convolution_bitcast_fusion.19), channel_id=1, source_target_pairs={{0,64},{64,0},{4,68},{68,4},{8,72},{72,8},{12,76},{76,12},{16,80},... | collective-permute-start | bytes 393224 | tf_op jit(solution)/shard_map/ppermute | solution.py:16
  104.6 1.1 convolution_bitcast_fusion.16
  105.8 0.6 collective-permute-start.6
  106.4 2.7 %collective-permute-done.4 = f32[256,128]{0,1:T(8,128)S(1)} collective-permute-done((f32[256,128]{0,1:T(8,128)S(1)}, f32[256,128]{0,1:T(8,128)S(1)}, u32[]{:S(2)}, u32[]{:S(2)}) %collective-permute-start.4) | collective-permute-done | bytes 131104 | tf_op jit(solution)/shard_map/ppermute | solution.py:16
  109.1 1.1 convolution_bitcast_fusion.18
  110.2 3.0 %collective-permute-start.5 = (f32[256,128]{0,1:T(8,128)S(1)}, f32[256,128]{0,1:T(8,128)S(1)}, u32[]{:S(2)}, u32[]{:S(2)}) collective-permute-start(f32[256,128]{0,1:T(8,128)S(1)} %convolution_bitcast_fusion.18), channel_id=1, source_target_pairs={{0,128},{128,0},{4,132},{132,4},{8,136},{136,8},{12,140},{140,12},... | collective-permute-start | bytes 393224 | tf_op jit(solution)/shard_map/ppermute | solution.py:16
  113.2 1.1 convolution_bitcast_fusion.14
  114.4 0.0 collective-permute-done.6
  114.4 3.5 %collective-permute-start.7 = (f32[256,128]{0,1:T(8,128)S(1)}, f32[256,128]{0,1:T(8,128)S(1)}, u32[]{:S(2)}, u32[]{:S(2)}) collective-permute-start(f32[256,128]{0,1:T(8,128)S(1)} %convolution_bitcast_fusion.14), channel_id=1, source_target_pairs={{0,32},{32,0},{4,36},{36,4},{8,40},{40,8},{12,44},{44,12},{16,48},... | collective-permute-start | bytes 393224 | tf_op jit(solution)/shard_map/ppermute | solution.py:16
  117.9 0.0 collective-permute-done.5
  117.9 0.3 fusion.5
  118.2 0.3 convolution_bitcast_fusion.15
  118.5 0.0 collective-permute-done.8
  118.5 5.4 %collective-permute-done.7 = f32[256,128]{0,1:T(8,128)S(1)} collective-permute-done((f32[256,128]{0,1:T(8,128)S(1)}, f32[256,128]{0,1:T(8,128)S(1)}, u32[]{:S(2)}, u32[]{:S(2)}) %collective-permute-start.7) | collective-permute-done | bytes 131104 | tf_op jit(solution)/shard_map/ppermute | solution.py:16
  123.8 0.3 fusion.6
  124.1 0.3 convolution_bitcast_fusion.11
  124.5 0.0 collective-permute-done.10
  124.5 0.0 collective-permute-done.9
  124.5 1.2 fusion.7
  125.7 1.4 fusion.4
  127.1 0.1 copy.18
  127.3 0.6 fusion.3
  127.9 0.0 all-gather.2.cloned.1.call-done
  127.9 6.3 %fusion.56 = f32[4,512,128]{2,1,0:T(8,128)S(1)} fusion(bf16[4,512,2048]{2,1,0:T(8,128)(2,1)} %param.10, bf16[4,2048,128]{2,1,0:T(8,128)(2,1)} %all-gather.2.cloned.1.call-done), kind=kOutput, calls=%fused_computation.85 | convolution fusion | flops 1073741824 | bytes 11534336 | tf_op jit(solution)/shard_map/nrk,nkc->nrc/dot_general | solution.py:81
  134.2 1.2 fusion.1
  (5 shorter events, 0.1 us)
Async XLA Ops:
  6.5 1.2 copy-start
  6.5 73.1 %copy-start.1 = (bf16[1,5,256,256]{3,2,1,0:T(8,128)(2,1)S(1)}, bf16[1,5,256,256]{3,2,1,0:T(8,128)(2,1)}, u32[]{:S(2)}) copy-start(bf16[1,5,256,256]{3,2,1,0:T(8,128)(2,1)} %param.16) | copy-start | bytes 1966084
  6.5 54.2 %all-reduce.2.cloned.1.call-start = ((), (), s32[]{:S(2)}) async-start(), calls=%async_computation.1 | async-start | bytes 1048576 | tf_op jit(solution)/shard_map/psum | solution.py:55
  10.1 117.7 %all-gather.2.cloned.1.call-start = ((), (), s32[]{:S(2)}) async-start(), calls=%async_computation | async-start | bytes 2621440 | tf_op jit(solution)/shard_map/all_gather | solution.py:84
  10.9 116.4 %copy-start.2 = (bf16[4,256,256]{2,1,0:T(8,128)(2,1)S(1)}, bf16[4,256,256]{2,1,0:T(8,128)(2,1)}, u32[]{:S(2)}) copy-start(bf16[4,256,256]{2,1,0:T(8,128)(2,1)} %param.12) | copy-start | bytes 1572868
  65.0 10.5 %copy-start.3 = (f32[256,128]{0,1:T(8,128)}, f32[256,128]{0,1:T(8,128)S(1)}, u32[]{:S(2)}) copy-start(f32[256,128]{0,1:T(8,128)S(1)} %convolution_bitcast_fusion.23) | copy-start | bytes 393220
  68.6 55.9 %collective-permute-start.10 = (f32[256,128]{0,1:T(8,128)}, f32[256,128]{0,1:T(8,128)}, u32[]{:S(2)}, u32[]{:S(2)}) collective-permute-start(f32[256,128]{0,1:T(8,128)} %convolution_bitcast_fusion.8), channel_id=1, source_target_pairs={{0,4},{4,0},{8,12},{12,8},{16,20},{20,16},{24,28},{28,24},{32,36},... | collective-permute-start | bytes 393224 | tf_op jit(solution)/shard_map/ppermute | solution.py:16
  68.6 3.5 %collective-permute-start = (f32[256,128]{0,1:T(8,128)S(1)}, f32[256,128]{0,1:T(8,128)S(1)}, u32[]{:S(2)}, u32[]{:S(2)}) collective-permute-start(f32[256,128]{0,1:T(8,128)S(1)} %convolution_bitcast_fusion.23), channel_id=1, source_target_pairs={{0,4},{4,0},{8,12},{12,8},{16,20},{20,16},{24,28},{28,24},{32,36},... | collective-permute-start | bytes 393224 | tf_op jit(solution)/shard_map/ppermute | solution.py:16
  72.1 3.4 %copy-start.4 = (f32[256,128]{0,1:T(8,128)}, f32[256,128]{0,1:T(8,128)S(1)}, u32[]{:S(2)}) copy-start(f32[256,128]{0,1:T(8,128)S(1)} %collective-permute-done) | copy-start | bytes 393220
  73.9 5.7 %collective-permute-start.1 = (f32[256,128]{0,1:T(8,128)}, f32[256,128]{0,1:T(8,128)}, u32[]{:S(2)}, u32[]{:S(2)}) collective-permute-start(f32[256,128]{0,1:T(8,128)} %convolution_bitcast_fusion.22), channel_id=1, source_target_pairs={{0,8},{8,0},{4,12},{12,4},{16,24},{24,16},{20,28},{28,20},{32,40},... | collective-permute-start | bytes 393224 | tf_op jit(solution)/shard_map/ppermute | solution.py:16
  80.8 8.4 %collective-permute-start.2 = (f32[256,128]{0,1:T(8,128)S(1)}, f32[256,128]{0,1:T(8,128)S(1)}, u32[]{:S(2)}, u32[]{:S(2)}) collective-permute-start(f32[256,128]{0,1:T(8,128)S(1)} %convolution_bitcast_fusion.21), channel_id=1, source_target_pairs={{0,16},{16,0},{4,20},{20,4},{8,24},{24,8},{12,28},{28,12},{32,48},... | collective-permute-start | bytes 393224 | tf_op jit(solution)/shard_map/ppermute | solution.py:16
  84.7 39.7 %collective-permute-start.9 = (f32[256,128]{0,1:T(8,128)S(1)}, f32[256,128]{0,1:T(8,128)S(1)}, u32[]{:S(2)}, u32[]{:S(2)}) collective-permute-start(f32[256,128]{0,1:T(8,128)S(1)} %convolution_bitcast_fusion.10), channel_id=1, source_target_pairs={{0,8},{8,0},{4,12},{12,4},{16,24},{24,16},{20,28},{28,20},{32,40},... | collective-permute-start | bytes 393224 | tf_op jit(solution)/shard_map/ppermute | solution.py:16
  89.5 13.4 %collective-permute-start.3 = (f32[256,128]{0,1:T(8,128)S(1)}, f32[256,128]{0,1:T(8,128)S(1)}, u32[]{:S(2)}, u32[]{:S(2)}) collective-permute-start(f32[256,128]{0,1:T(8,128)S(1)} %convolution_bitcast_fusion.20), channel_id=1, source_target_pairs={{0,32},{32,0},{4,36},{36,4},{8,40},{40,8},{12,44},{44,12},{16,48},... | collective-permute-start | bytes 393224 | tf_op jit(solution)/shard_map/ppermute | solution.py:16
  96.6 21.9 %collective-permute-start.8 = (f32[256,128]{0,1:T(8,128)S(1)}, f32[256,128]{0,1:T(8,128)S(1)}, u32[]{:S(2)}, u32[]{:S(2)}) collective-permute-start(f32[256,128]{0,1:T(8,128)S(1)} %convolution_bitcast_fusion.12), channel_id=1, source_target_pairs={{0,16},{16,0},{4,20},{20,4},{8,24},{24,8},{12,28},{28,12},{32,48},... | collective-permute-start | bytes 393224 | tf_op jit(solution)/shard_map/ppermute | solution.py:16
  103.0 6.0 %collective-permute-start.4 = (f32[256,128]{0,1:T(8,128)S(1)}, f32[256,128]{0,1:T(8,128)S(1)}, u32[]{:S(2)}, u32[]{:S(2)}) collective-permute-start(f32[256,128]{0,1:T(8,128)S(1)} %convolution_bitcast_fusion.19), channel_id=1, source_target_pairs={{0,64},{64,0},{4,68},{68,4},{8,72},{72,8},{12,76},{76,12},{16,80},... | collective-permute-start | bytes 393224 | tf_op jit(solution)/shard_map/ppermute | solution.py:16
  105.8 8.6 %collective-permute-start.6 = (f32[256,128]{0,1:T(8,128)S(1)}, f32[256,128]{0,1:T(8,128)S(1)}, u32[]{:S(2)}, u32[]{:S(2)}) collective-permute-start(f32[256,128]{0,1:T(8,128)S(1)} %convolution_bitcast_fusion.16), channel_id=1, source_target_pairs={{0,64},{64,0},{4,68},{68,4},{8,72},{72,8},{12,76},{76,12},{16,80},... | collective-permute-start | bytes 393224 | tf_op jit(solution)/shard_map/ppermute | solution.py:16
  110.2 7.6 %collective-permute-start.5 = (f32[256,128]{0,1:T(8,128)S(1)}, f32[256,128]{0,1:T(8,128)S(1)}, u32[]{:S(2)}, u32[]{:S(2)}) collective-permute-start(f32[256,128]{0,1:T(8,128)S(1)} %convolution_bitcast_fusion.18), channel_id=1, source_target_pairs={{0,128},{128,0},{4,132},{132,4},{8,136},{136,8},{12,140},{140,12},... | collective-permute-start | bytes 393224 | tf_op jit(solution)/shard_map/ppermute | solution.py:16
  114.4 9.4 %collective-permute-start.7 = (f32[256,128]{0,1:T(8,128)S(1)}, f32[256,128]{0,1:T(8,128)S(1)}, u32[]{:S(2)}, u32[]{:S(2)}) collective-permute-start(f32[256,128]{0,1:T(8,128)S(1)} %convolution_bitcast_fusion.14), channel_id=1, source_target_pairs={{0,32},{32,0},{4,36},{36,4},{8,40},{40,8},{12,44},{44,12},{16,48},... | collective-permute-start | bytes 393224 | tf_op jit(solution)/shard_map/ppermute | solution.py:16
Sparse Core Ops, SparseCore 0:
  10.3 50.3 all-reduce.1
  62.5 33.4 all-gather.1
where the time goes:
time: 143 us; the launch traced here: 142 us
  waiting for transfers between devices  70.3 us (49%)
  matrix products  35.7 us (25%)
  starting transfers between devices  21 us (15%)
  between operations  13.7 us (10%)
  local copies, waits for them, and re-layouts  1.59 us (1%)
    psum x1, waiting for transfers between devices, shards(): skel_leaf = lax.psum(partial_skel, 'row')  49.8 us
    ppermute x11, starting transfers between devices, swapped(): return lax.ppermute(block, axis, route)  21 us
    ppermute x11, waiting for transfers between devices, swapped(): return lax.ppermute(block, axis, route)  19.7 us
    dot_general x5, matrix products, shards(): outgoing = jnp.dot(couple_mats[height].T, current, precision=precise)  6.61 us
    dot_general x1, matrix products, shards(): jnp.einsum('nrk,nkc->nrc', near_blocks, lax.all_gather(fields, 'row', axi...  6.3 us
    dot_general x5, matrix products, shards(): lifted = jnp.dot(lift_mats[height].T, current, precision=precise)  4.64 us
    dot_general x2, matrix products, couple_pairs(): to_right = jnp.einsum('psr,psc->prc', mats32, left_skel, precision=precise)  3.25 us
    dot_general x2, matrix products, lift(): jnp.einsum('nrs,nrc->nsc', mats.astype(jnp.float32), skel, precision=prec...  3.1 us
  transfers between devices with their start and end apart: 13, of which 6 were waited for; matrix products, arithmetic and copies ran while one was open for 18% of the time, Pallas kernels for 0%

commit v1 on v0

v1 whole, which is shorter than its diff:
```python
import functools

import jax
import jax.numpy as jnp
from jax import lax
from jax.experimental import pallas as pl
from jax.experimental.pallas import tpu as pltpu
from jax.sharding import PartitionSpec as P

bf16 = jnp.bfloat16
f32 = jnp.float32
precise = lax.Precision.HIGHEST
PARTNERS = (1, 2, 4, 12, 16, 48)


def exchange(value, axis, mask):
    count = lax.axis_size(axis)
    return lax.ppermute(value, axis, [(i, i ^ mask) for i in range(count)])


def shifted(value, step):
    count = lax.axis_size("row")
    return lax.ppermute(value, "row", [(i, (i + step) % count) for i in range(count)])


def times(values, mats):
    return lax.dot_general(
        values, mats.astype(f32), (((1,), (0,)), ((), ())), precision=precise
    )


def times_t(values, mats):
    return lax.dot_general(
        values, mats.astype(f32), (((1,), (1,)), ((), ())), precision=precise
    )


def split_dot(values, mats, contract):
    rows = values.shape[0]
    high = values.astype(bf16)
    low = (values - high.astype(f32)).astype(bf16)
    both = lax.dot_general(
        jnp.concatenate([high, low], axis=0),
        mats,
        (((1,), (contract,)), ((), ())),
        preferred_element_type=f32,
    )
    return both[:rows] + both[rows:]


def after(value, *others):
    return lax.optimization_barrier((value,) + others)[0]


def hold(signal, *values, flops=1 << 24):
    anywhere = pl.BlockSpec(memory_space=pl.ANY)
    return pl.pallas_call(
        lambda *refs: None,
        out_shape=tuple(jax.ShapeDtypeStruct(v.shape, v.dtype) for v in values),
        in_specs=[anywhere] * (1 + len(values)),
        out_specs=(anywhere,) * len(values),
        input_output_aliases={1 + i: i for i in range(len(values))},
        compiler_params=pltpu.CompilerParams(vmem_limit_bytes=16 << 20),
        cost_estimate=pl.CostEstimate(flops=flops, bytes_accessed=0, transcendentals=0),
    )(signal, *values)


def two_terms(values):
    high = lax.reduce_precision(values, 8, 7)
    return high.astype(bf16), (values - high).astype(bf16)


def gather_kernel(
    half,
    fields,
    basis,
    lt,
    mt,
    keep,
    send,
    side_keep,
    side_send,
    f_buf,
    basis_out,
    lt_out,
    mt_out,
    scratch,
    sems,
):
    f_copy = pltpu.make_async_copy(fields, f_buf, sems.at[0])
    b_copies = [
        pltpu.make_async_copy(
            basis.at[pl.ds(2 * pair, 2)], basis_out.at[pl.ds(2 * pair, 2)], sems.at[1 + pair]
        )
        for pair in range(2)
    ]
    lt_copy = pltpu.make_async_copy(lt, lt_out, sems.at[3])
    mt_copy = pltpu.make_async_copy(mt, mt_out, sems.at[4])
    for copy in (f_copy, *b_copies, lt_copy, mt_copy):
        copy.start()
    mine = pl.ds(pl.multiple_of(half[0] * 64, 64), 64)
    other = pl.ds(pl.multiple_of(64 - half[0] * 64, 64), 64)
    f_copy.wait()
    for n in range(4):
        if n % 2 == 0:
            b_copies[n // 2].wait()
        scratch[n] = lax.dot_general(
            f_buf[n], basis_out[n], (((0,), (0,)), ((), ())), preferred_element_type=f32
        )
    lt_copy.wait()
    mt_copy.wait()
    current = None
    for pair in range(2):
        mid = split_dot(scratch[2 * pair], lt_out[2 * pair], 0) + split_dot(
            scratch[2 * pair + 1], lt_out[2 * pair + 1], 0
        )
        lifted = split_dot(mid, mt_out[pair], 0)
        current = lifted if current is None else current + lifted
    scratch[4] = current
    keep[...] = scratch[4, mine, :]
    send[...] = scratch[4, other, :]
    for n in range(4):
        side_keep[n] = scratch[n, mine, :]
        side_send[n] = scratch[n, other, :].astype(bf16)


def gather_skeletons(half, fields, basis, lt, mt):
    vmem = pl.BlockSpec(memory_space=pltpu.VMEM)
    return pl.pallas_call(
        gather_kernel,
        out_shape=(
            jax.ShapeDtypeStruct((64, 256), f32),
            jax.ShapeDtypeStruct((64, 256), f32),
            jax.ShapeDtypeStruct((4, 64, 256), f32),
            jax.ShapeDtypeStruct((4, 64, 256), bf16),
        ),
        in_specs=[pl.BlockSpec(memory_space=pltpu.SMEM)] + [pl.BlockSpec(memory_space=pl.ANY)] * 4,
        out_specs=(vmem,) * 4,
        scratch_shapes=[
            pltpu.VMEM((4, 512, 128), bf16),
            pltpu.VMEM((4, 512, 256), bf16),
            pltpu.VMEM((4, 256, 256), bf16),
            pltpu.VMEM((2, 256, 256), bf16),
            pltpu.VMEM((5, 128, 256), f32),
            pltpu.SemaphoreType.DMA((5,)),
        ],
        compiler_params=pltpu.CompilerParams(vmem_limit_bytes=54528 << 10),
        cost_estimate=pl.CostEstimate(
            flops=2 * 4 * 512 * 256 * 128, bytes_accessed=3 << 20, transcendentals=0
        ),
    )(half, fields, basis, lt, mt)


def stage_kernel(keep, ct, cc, lc, mc, joint, crown, lc_out, mc_out, sems):
    copies = [
        pltpu.make_async_copy(ct.at[0], joint.at[:, :, pl.ds(0, 256)], sems.at[0]),
        pltpu.make_async_copy(
            cc.at[0, pl.ds(0, 5)], joint.at[:, :, pl.ds(256, 256)], sems.at[1]
        ),
        pltpu.make_async_copy(cc.at[0, 5], crown, sems.at[2]),
        pltpu.make_async_copy(lc, lc_out, sems.at[3]),
        pltpu.make_async_copy(mc, mc_out, sems.at[4]),
    ]
    for copy in copies:
        copy.start()
    for copy in copies:
        copy.wait()


def stage_mats(keep, ct, cc, lc, mc):
    vmem = pl.BlockSpec(memory_space=pltpu.VMEM)
    return pl.pallas_call(
        stage_kernel,
        out_shape=(
            jax.ShapeDtypeStruct((5, 256, 512), bf16),
            jax.ShapeDtypeStruct((256, 256), bf16),
            jax.ShapeDtypeStruct((2, 256, 256), bf16),
            jax.ShapeDtypeStruct((1, 256, 256), bf16),
        ),
        in_specs=[pl.BlockSpec(memory_space=pl.ANY)] * 5,
        out_specs=(vmem,) * 4,
        scratch_shapes=[pltpu.SemaphoreType.DMA((5,))],
        compiler_params=pltpu.CompilerParams(vmem_limit_bytes=16 << 20),
        cost_estimate=pl.CostEstimate(flops=0, bytes_accessed=4 << 20, transcendentals=0),
    )(keep, ct, cc, lc, mc)


def near_kernel(offsets, pieces, started, place, near, signal, *refs):
    parts, refs = refs[:pieces], refs[pieces:]
    out = refs[-1]
    for n in range(4):
        total = refs[0][n] if started else None
        for i, offset in enumerate(offsets):
            column = pl.multiple_of(lax.rem(place[0] + offset, 4) * 512, 512)
            part = parts[i][n] if len(offsets) == pieces else parts[n // 2][n % 2]
            term = jnp.dot(near[n, :, pl.ds(column, 512)], part, preferred_element_type=f32)
            total = term if total is None else total + term
        out[n] = total


def near_product(place, near, signal, offsets, parts, so_far=None):
    vmem = pl.BlockSpec(memory_space=pltpu.VMEM)
    extra = () if so_far is None else (so_far,)
    return pl.pallas_call(
        functools.partial(near_kernel, offsets, len(parts), bool(extra)),
        out_shape=jax.ShapeDtypeStruct((4, 512, 128), f32),
        in_specs=[pl.BlockSpec(memory_space=pltpu.SMEM), vmem, pl.BlockSpec(memory_space=pl.ANY)]
        + [vmem] * (len(parts) + len(extra)),
        out_specs=vmem,
        compiler_params=pltpu.CompilerParams(vmem_limit_bytes=24 << 20),
        cost_estimate=pl.CostEstimate(
            flops=1 << 31, bytes_accessed=1 << 12, transcendentals=0
        ),
    )(place, near, signal, *parts, *extra)


def side_kernel(signal, own, got, lt, lc, mc, out, out_low, skel):
    for n in range(4):
        skel[n] = own[n] + got[n].astype(f32)
    mid = [
        split_dot(skel[2 * pair], lt[2 * pair], 0)
        + split_dot(skel[2 * pair + 1], lt[2 * pair + 1], 0)
        for pair in range(2)
    ]
    for pair in range(2):
        pot_mid = split_dot(mid[1 - pair], mc[0], 1 - pair)
        for k in range(2):
            n = 2 * pair + k
            out[n] = split_dot(skel[2 * pair + 1 - k], lc[pair], 1 - k) + split_dot(
                pot_mid, lt[n], 1
            )
            out_low[n] = out[n].astype(bf16)


def side_potentials(signal, own, got, lt, lc, mc):
    vmem = pl.BlockSpec(memory_space=pltpu.VMEM)
    return pl.pallas_call(
        side_kernel,
        out_shape=(
            jax.ShapeDtypeStruct((4, 64, 256), f32),
            jax.ShapeDtypeStruct((4, 64, 256), bf16),
        ),
        in_specs=[pl.BlockSpec(memory_space=pl.ANY)] + [vmem] * 5,
        out_specs=(vmem,) * 2,
        scratch_shapes=[pltpu.VMEM((4, 64, 256), f32)],
        compiler_params=pltpu.CompilerParams(vmem_limit_bytes=16 << 20),
        cost_estimate=pl.CostEstimate(flops=1 << 24, bytes_accessed=1 << 12, transcendentals=0),
    )(signal, own, got, lt, lc, mc)


def final_kernel(
    half,
    own,
    other,
    side_own,
    side_other,
    mt,
    lt,
    basis,
    near,
    out,
    pot,
    side,
    buf,
    sems,
):
    mine = pl.ds(pl.multiple_of(half[0] * 64, 64), 64)
    rest = pl.ds(pl.multiple_of(64 - half[0] * 64, 64), 64)
    pot[mine, :] = own[...]
    pot[rest, :] = other[...]
    for n in range(4):
        side[n, mine, :] = side_own[n]
        side[n, rest, :] = side_other[n].astype(f32)
    copies = []
    for pair in range(2):
        mid = split_dot(pot[...], mt[pair], 1)
        for k in range(2):
            n = 2 * pair + k
            low = (split_dot(mid, lt[n], 1) + side[n]).astype(bf16)
            far = lax.dot_general(
                basis[n], low, (((1,), (1,)), ((), ())), preferred_element_type=f32
            )
            buf[n] = (near[n] + far).astype(bf16)
            copies.append(pltpu.make_async_copy(buf.at[n], out.at[n], sems.at[n]))
            copies[n].start()
    for copy in copies:
        copy.wait()


def final_product(half, own, other, side_own, side_other, mt, lt, basis, near):
    vmem = pl.BlockSpec(memory_space=pltpu.VMEM)
    return pl.pallas_call(
        final_kernel,
        out_shape=jax.ShapeDtypeStruct((4, 512, 128), bf16),
        in_specs=[pl.BlockSpec(memory_space=pltpu.SMEM)] + [vmem] * 8,
        out_specs=pl.BlockSpec(memory_space=pl.ANY),
        scratch_shapes=[
            pltpu.VMEM((128, 256), f32),
            pltpu.VMEM((4, 128, 256), f32),
            pltpu.VMEM((4, 512, 128), bf16),
            pltpu.SemaphoreType.DMA((4,)),
        ],
        compiler_params=pltpu.CompilerParams(vmem_limit_bytes=16 << 20),
        cost_estimate=pl.CostEstimate(
            flops=2 * 4 * 512 * 256 * 128, bytes_accessed=4 << 20, transcendentals=0
        ),
    )(half, own, other, side_own, side_other, mt, lt, basis, near)


def shards(
    fields,
    near_blocks,
    leaf_basis,
    leaf_transfer,
    mid_transfer,
    leaf_couple,
    mid_couple,
    cross_transfer,
    cross_couple,
):
    place = lax.axis_index("row")
    first_core = (lax.axis_index("leaf") & 1) == 0
    half = ((place ^ (place >> 1)) & 1).reshape(1)
    place = place.reshape(1)

    keep, send, side_keep, side_send = gather_skeletons(
        half, fields, leaf_basis, leaf_transfer, mid_transfer
    )
    basis, lt, mt = leaf_basis, leaf_transfer, mid_transfer
    joint, crown, lc, mc = stage_mats(keep, cross_transfer, cross_couple, leaf_couple, mid_couple)
    with jax.named_scope("row_sum"):
        current = keep + exchange(send, "row", 1)
        (side_send,) = hold(current, side_send)
        got_side = exchange(side_send, "row", 1)
        current = current + exchange(current, "row", 3)

    with jax.named_scope("level0"):
        both = times(current, joint[0])
        lifted = both[:, :256]
        mine = jnp.where(first_core, lifted[:32], lifted[32:])
        other = jnp.where(first_core, lifted[32:], lifted[:32])
        payload = jnp.concatenate([other, both[:, 256:]], axis=0)
        with jax.named_scope("side2"):
            (got_side,) = hold(payload, got_side)
            skel = side_keep + got_side.astype(f32)
            across_side = exchange(skel.astype(bf16), "row", 3)
        got = exchange(payload, "leaf", 1)
        current = mine + got[:32]
        incoming = [got[32:]]

    def prepare(level, current):
        both = times(current, joint[level])
        lifted = both[:, :256]
        payload = jnp.concatenate([*two_terms(lifted), both[:, 256:].astype(bf16)], axis=1)
        return lifted, payload

    def rise(level, lifted, payload):
        got = exchange(payload, "leaf", PARTNERS[level]).astype(f32)
        incoming.append(got[:, 512:])
        return lifted + (got[:, :256] + got[:, 256:512])

    with jax.named_scope("level1"):
        lifted, payload = prepare(1, current)
        with jax.named_scope("ring"):
            ready = after(fields, payload)
            from_left = shifted(ready, 1)
            from_right = shifted(ready, -1)
        current = rise(1, lifted, payload)
    with jax.named_scope("level2"):
        lifted, payload = prepare(2, current)
        across_side, payload = lax.optimization_barrier((across_side, payload))
        with jax.named_scope("near"):
            near = near_product(place, near_blocks, payload, (0,), (fields,))
        with jax.named_scope("side"):
            side, side_send = side_potentials(payload, skel, across_side, lt, lc, mc)
        with jax.named_scope("path"):
            (steps,) = hold(payload, joint[1:5, :, :256])
            path = steps[0].astype(f32)
            for level in (1, 2, 3):
                path = times(path, steps[level])
        current = rise(2, lifted, payload)
    with jax.named_scope("level3"):
        lifted, payload = prepare(3, current)
        near, side, path, payload = lax.optimization_barrier((near, side, path, payload))
        with jax.named_scope("side3"):
            (side_send,) = hold(payload, side_send, flops=1 << 32)
            side_other = exchange(side_send, "row", 1)
        current = rise(3, lifted, payload)
    with jax.named_scope("level4"):
        lifted, payload = prepare(4, current)
        from_left, from_right, side_send, payload = lax.optimization_barrier(
            (from_left, from_right, side_send, payload)
        )
        with jax.named_scope("across"):
            from_left, from_right = hold(payload, from_left, from_right)
            across0 = shifted(from_left[:2], 1)
            across1 = shifted(from_right[2:], -1)
        current = rise(4, lifted, payload)
    with jax.named_scope("level5"):
        payload = times(current, crown).astype(bf16)
        side_other, payload = lax.optimization_barrier((side_other, payload))
        (tail,) = hold(payload, incoming[4])
        for level in (3, 2, 1):
            tail = times_t(tail, joint[level, :, :256]) + incoming[level]
        potential = exchange(payload, "leaf", PARTNERS[5]).astype(f32)

    with jax.named_scope("down"):
        tail, potential = lax.optimization_barrier((tail, potential))
        potential = times_t(potential, path) + tail
        (side,) = hold(potential, side, flops=1 << 32)
        other = exchange(potential, "leaf", 1)
        top = jnp.where(first_core, potential, other)
        bottom = jnp.where(first_core, other, potential)
        potential = times_t(jnp.concatenate([top, bottom]), joint[0, :, :256]) + incoming[0]
        across0, across1, side, potential = lax.optimization_barrier(
            (across0, across1, side, potential)
        )
        with jax.named_scope("near"):
            near = near_product(
                place, near_blocks, potential, (3, 1), (from_left, from_right), near
            )
            near = near_product(place, near_blocks, potential, (2,), (across0, across1), near)
        other = exchange(potential, "row", 1)
    with jax.named_scope("final"):
        return final_product(
            half, potential, other, side, side_other, mt, lt, basis, near
        )


def solution(mesh):
    return jax.shard_map(
        shards,
        mesh=mesh,
        in_specs=(
            P("leaf", "row", None),
            P("leaf", "row", None),
            P("leaf", "row", None),
            P("leaf", None, None),
            P("leaf", None, None),
            P("leaf", None, None),
            P("leaf", None, None),
            P("leaf", None, None, None),
            P("leaf", None, None, None),
        ),
        out_specs=P("leaf", "row", None),
        check_vma=False,
    )
```

time: 143 us -> 58.5 us (0.41)
  the two profiles are of different devices: /device:TPU:4 before, /device:TPU:1 now
where the time goes in v1:
time: 58.5 us; the launch traced here: 58.3 us
  starting transfers between devices  35.9 us (61%)
  waiting for transfers between devices  9.43 us (16%)
  Pallas kernels  8.29 us (14%)
  matrix products  3.51 us (6%)
  between operations  0.6 us (1%)
    ppermute x13, starting transfers between devices, exchange(): return lax.ppermute(value, axis, [(i, i ^ mask) for i in range(count)])  30.3 us
    ppermute x13, waiting for transfers between devices, exchange(): return lax.ppermute(value, axis, [(i, i ^ mask) for i in range(count)])  8.85 us
    ppermute x4, starting transfers between devices, shifted(): lax.ppermute(value, 'row', [(i, (i + step) % count) for i in range(count)])  5.51 us
    pallas_call x3, Pallas kernels, near_product(): pl.pallas_call(functools.partial(near_kernel, offsets, len(parts), bool(e...  2.7 us
    pallas_call x1, Pallas kernels, gather_skeletons(): pl.pallas_call(gather_kernel, out_shape=(jax.ShapeDtypeStruct((64, 256),...  2.45 us
    dot_general x9, matrix products, times(): lax.dot_general(values, mats.astype(f32), (((1,), (0,)), ((), ())), preci...  2.11 us
    pallas_call x1, Pallas kernels, final_product(): pl.pallas_call(final_kernel, out_shape=jax.ShapeDtypeStruct((4, 512, 128)...  1.92 us
    dot_general x5, matrix products, times_t(): lax.dot_general(values, mats.astype(f32), (((1,), (1,)), ((), ())), preci...  1.4 us
  transfers between devices with their start and end apart: 17, of which 9 were waited for; matrix products, arithmetic and copies ran while one was open for 6% of the time, Pallas kernels for 7%

profile of v1, /device:TPU:1, one launch (start us, length us, event | category | flops | bytes accessed | tf_op | source)
XLA Modules:
  0.0 58.3 jit_solution(3665132161616154009)
XLA Ops:
  0.0 0.0 copy-start.5
  0.0 2.4 %shard_map.91 = (f32[64,256]{1,0:T(8,128)S(1)}, f32[64,256]{1,0:T(8,128)S(1)}, f32[4,64,256]{2,1,0:T(8,128)S(1)}, bf16[4,64,256]{2,1,0:T(8,128)(2,1)S(1)}) custom-call(s32[1]{0:T(128)} %bitcast.half, bf16[4,512,128]{2,1,0:T(8,128)(2,1)} %refs_0_.1, bf16[4,512,256]{2,1,0:T(8,128)(2,1)} %basis.3, bf16[4,256,256]{2,1,0:T(8,128)(2,1)} %lt.5, bf16[2,256,256]{2,1,0:T(8,128)(2,1)} %mt.3), custom_call_target="tpu_custom_call" | custom-call | flops 134217728 | bytes 3145728 | tf_op jit(solution)/shard_map/pallas_call | solution.py:129
  2.5 2.1 %collective-permute-start = (f32[64,256]{1,0:T(8,128)S(1)}, f32[64,256]{1,0:T(8,128)S(1)}, u32[]{:S(2)}, u32[]{:S(2)}) collective-permute-start(f32[64,256]{1,0:T(8,128)S(1)} %get-tuple-element.36), channel_id=1, source_target_pairs={{0,1},{1,0},{2,3},{3,2},{4,5},{5,4},{6,7},{7,6},{8,9},{9,8},{10,11... | collective-permute-start | bytes 196616 | tf_op jit(solution)/shard_map/row_sum/ppermute | solution.py:18
  4.6 1.7 %collective-permute-done = f32[64,256]{1,0:T(8,128)S(1)} collective-permute-done((f32[64,256]{1,0:T(8,128)S(1)}, f32[64,256]{1,0:T(8,128)S(1)}, u32[]{:S(2)}, u32[]{:S(2)}) %collective-permute-start) | collective-permute-done | bytes 65568 | tf_op jit(solution)/shard_map/row_sum/ppermute | solution.py:18
  6.3 2.8 %collective-permute-start.1 = (f32[64,256]{1,0:T(8,128)S(1)}, f32[64,256]{1,0:T(8,128)S(1)}, u32[]{:S(2)}, u32[]{:S(2)}) collective-permute-start(f32[64,256]{1,0:T(8,128)S(1)} %add.51.refs_0_), channel_id=1, source_target_pairs={{0,3},{1,2},{2,1},{3,0},{4,7},{5,6},{6,5},{7,4},{8,11},{9,10},{10,... | collective-permute-start | bytes 196616 | tf_op jit(solution)/shard_map/row_sum/ppermute | solution.py:18
  9.1 0.0 copy-done.7
  9.1 0.0 copy-start
  9.1 0.5 shard_map.92
  9.6 0.1 collective-permute-start.5
  9.7 1.0 %collective-permute-done.1 = f32[64,256]{1,0:T(8,128)S(1)} collective-permute-done((f32[64,256]{1,0:T(8,128)S(1)}, f32[64,256]{1,0:T(8,128)S(1)}, u32[]{:S(2)}, u32[]{:S(2)}) %collective-permute-start.1) | collective-permute-done | bytes 65568 | tf_op jit(solution)/shard_map/row_sum/ppermute | solution.py:18
  10.7 0.3 fusion.8
  11.1 5.0 %collective-permute-start.2 = (f32[96,256]{1,0:T(8,128)S(1)}, f32[96,256]{1,0:T(8,128)S(1)}, u32[]{:S(2)}, u32[]{:S(2)}) collective-permute-start(f32[96,256]{1,0:T(8,128)S(1)} %pad_maximum_fusion.refs_0_), channel_id=1, source_target_pairs={{0,4},{4,0},{8,12},{12,8},{16,20},{20,16},{24,28},{28,24},{32,36},... | collective-permute-start | bytes 294920 | tf_op jit(solution)/shard_map/level0/ppermute | solution.py:18
  16.1 0.0 collective-permute-done.5.refs_1_
  16.1 0.9 %collective-permute-done.2 = f32[96,256]{1,0:T(8,128)S(1)} collective-permute-done((f32[96,256]{1,0:T(8,128)S(1)}, f32[96,256]{1,0:T(8,128)S(1)}, u32[]{:S(2)}, u32[]{:S(2)}) %collective-permute-start.2) | collective-permute-done | bytes 98336 | tf_op jit(solution)/shard_map/level0/ppermute | solution.py:18
  17.0 0.2 fusion.6
  17.3 0.1 collective-permute-start.7
  17.4 2.5 %collective-permute-start.6 = (bf16[4,64,256]{2,1,0:T(8,128)(2,1)S(1)}, bf16[4,64,256]{2,1,0:T(8,128)(2,1)S(1)}, u32[]{:S(2)}, u32[]{:S(2)}) collective-permute-start(bf16[4,64,256]{2,1,0:T(8,128)(2,1)S(1)} %get-tuple-element.65), channel_id=1, source_target_pairs={{0,3},{1,2},{2,1},{3,0},{4,7},{5,6},{6,5},{7,4},{8,11},{9,10},{10,... | collective-permute-start | bytes 393224 | tf_op jit(solution)/shard_map/level0/side2/ppermute | solution.py:18
  19.9 0.0 copy-done.3
  19.9 0.0 collective-permute-start.3
  19.9 2.7 %collective-permute-start.4 = (bf16[4,512,128]{2,1,0:T(8,128)(2,1)S(1)}, bf16[4,512,128]{2,1,0:T(8,128)(2,1)S(1)}, u32[]{:S(2)}, u32[]{:S(2)}) collective-permute-start(bf16[4,512,128]{2,1,0:T(8,128)(2,1)S(1)} %copy-done.3), channel_id=1, source_target_pairs={{0,3},{1,0},{2,1},{3,2},{4,7},{5,4},{6,5},{7,6},{8,11},{9,8},{10,9... | collective-permute-start | bytes 1572872 | tf_op jit(solution)/shard_map/level1/ring/ppermute | solution.py:23
  22.5 0.0 collective-permute-done.7
  22.6 0.2 fusion.4
  22.9 0.0 collective-permute-done.6.got
  22.9 3.1 %collective-permute-start.8 = (bf16[32,768]{1,0:T(8,128)(2,1)S(1)}, bf16[32,768]{1,0:T(8,128)(2,1)S(1)}, u32[]{:S(2)}, u32[]{:S(2)}) collective-permute-start(bf16[32,768]{1,0:T(8,128)(2,1)S(1)} %pad_maximum_fusion.2.signal.refs_0_), channel_id=1, source_target_pairs={{0,16},{4,20},{8,24},{12,28},{16,0},{20,4},{24,8},{28,12},{32,48},... | collective-permute-start | bytes 147464 | tf_op jit(solution)/shard_map/level2/ppermute | solution.py:18
  25.9 0.2 fusion.17
  26.1 0.3 fusion.16
  26.4 0.3 fusion.15
  26.7 0.0 copy-start.1
  26.7 0.7 %near.6.refs_2_ = f32[4,512,128]{2,1,0:T(8,128)S(1)} custom-call(s32[1]{0:T(128)} %bitcast.3.place, bf16[4,512,2048]{2,1,0:T(8,128)(2,1)S(1)} %copy-done, bf16[32,768]{1,0:T(8,128)(2,1)S(1)} %pad_maximum_fusion.2.signal.refs_0_, bf16[4,512,128]{2,1,0:T(8,128)(2,1)S(1)} %copy-done.3), custom_call_target="tpu_custom_call" | custom-call | flops 2147483648 | bytes 4096 | tf_op jit(solution)/shard_map/level2/near/pallas_call | solution.py:204
  27.4 0.3 copy-done.1
  27.7 0.7 %side.1 = (f32[4,64,256]{2,1,0:T(8,128)S(1)}, bf16[4,64,256]{2,1,0:T(8,128)(2,1)S(1)}) custom-call(bf16[32,768]{1,0:T(8,128)(2,1)S(1)} %pad_maximum_fusion.2.signal.refs_0_, f32[4,64,256]{2,1,0:T(8,128)S(1)} %get-tuple-element.66.own, bf16[4,64,256]{2,1,0:T(8,128)(2,1)S(1)} %collective-permute-done.6.got, bf16[4,256,256]{2,1,0:T(8,128)(2,1)S(1)} %copy-done.1, ...), custom_call_target="tpu_custom_call" | custom-call | flops 16777216 | bytes 4096 | tf_op jit(solution)/shard_map/level2/side/pallas_call | solution.py:237
  28.4 0.0 collective-permute-done.8
  28.5 0.2 fusion.2
  28.8 3.8 %collective-permute-start.9 = (bf16[32,768]{1,0:T(8,128)(2,1)S(1)}, bf16[32,768]{1,0:T(8,128)(2,1)S(1)}, u32[]{:S(2)}, u32[]{:S(2)}) collective-permute-start(bf16[32,768]{1,0:T(8,128)(2,1)S(1)} %pad_maximum_fusion.3.refs_0_), channel_id=1, source_target_pairs={{0,48},{4,52},{8,56},{12,60},{16,32},{20,36},{24,40},{28,44},{32,1... | collective-permute-start | bytes 147464 | tf_op jit(solution)/shard_map/level3/ppermute | solution.py:18
  32.6 1.6 %collective-permute-done.9 = bf16[32,768]{1,0:T(8,128)(2,1)S(1)} collective-permute-done((bf16[32,768]{1,0:T(8,128)(2,1)S(1)}, bf16[32,768]{1,0:T(8,128)(2,1)S(1)}, u32[]{:S(2)}, u32[]{:S(2)}) %collective-permute-start.9) | collective-permute-done | bytes 49184 | tf_op jit(solution)/shard_map/level3/ppermute | solution.py:18
  34.2 0.2 fusion
  34.5 0.6 collective-permute-done.3.refs_1_
  35.0 0.0 collective-permute-done.4.refs_2_
  35.0 1.3 %collective-permute-start.13 = (bf16[32,768]{1,0:T(8,128)(2,1)S(1)}, bf16[32,768]{1,0:T(8,128)(2,1)S(1)}, u32[]{:S(2)}, u32[]{:S(2)}) collective-permute-start(bf16[32,768]{1,0:T(8,128)(2,1)S(1)} %pad_maximum_fusion.4.refs_0_), channel_id=1, source_target_pairs={{0,64},{4,68},{8,72},{12,76},{16,80},{20,84},{24,88},{28,92},{32,9... | collective-permute-start | bytes 147464 | tf_op jit(solution)/shard_map/level4/ppermute | solution.py:18
  36.3 0.0 collective-permute-start.12
  36.4 1.5 %collective-permute-start.10 = (bf16[2,512,128]{2,1,0:T(8,128)(2,1)S(1)}, bf16[2,512,128]{2,1,0:T(8,128)(2,1)S(1)}, u32[]{:S(2)}, u32[]{:S(2)}) collective-permute-start(bf16[2,512,128]{2,1,0:T(8,128)(2,1)S(1)} %slice.160), channel_id=1, source_target_pairs={{0,1},{1,2},{2,3},{3,0},{4,5},{5,6},{6,7},{7,4},{8,9},{9,10},{10,1... | collective-permute-start | bytes 786440 | tf_op jit(solution)/shard_map/level4/across/ppermute | solution.py:23
  37.9 1.3 %collective-permute-start.11 = (bf16[2,512,128]{2,1,0:T(8,128)(2,1)S(1)}, bf16[2,512,128]{2,1,0:T(8,128)(2,1)S(1)}, u32[]{:S(2)}, u32[]{:S(2)}) collective-permute-start(bf16[2,512,128]{2,1,0:T(8,128)(2,1)S(1)} %slice.161), channel_id=1, source_target_pairs={{0,3},{1,0},{2,1},{3,2},{4,7},{5,4},{6,5},{7,6},{8,11},{9,8},{10,9... | collective-permute-start | bytes 786440 | tf_op jit(solution)/shard_map/level4/across/ppermute | solution.py:23
  39.2 0.0 collective-permute-done.13
  39.2 0.2 convolution_convert_fusion.refs_0_
  39.4 0.7 %collective-permute-done.12.side_other = bf16[4,64,256]{2,1,0:T(8,128)(2,1)S(1)} collective-permute-done((bf16[4,64,256]{2,1,0:T(8,128)(2,1)S(1)}, bf16[4,64,256]{2,1,0:T(8,128)(2,1)S(1)}, u32[]{:S(2)}, u32[]{:S(2)}) %collective-permute-start.12) | collective-permute-done | bytes 131104 | tf_op jit(solution)/shard_map/level3/side3/ppermute | solution.py:18
  40.1 1.9 %collective-permute-start.14 = (bf16[32,256]{1,0:T(8,128)(2,1)S(1)}, bf16[32,256]{1,0:T(8,128)(2,1)S(1)}, u32[]{:S(2)}, u32[]{:S(2)}) collective-permute-start(bf16[32,256]{1,0:T(8,128)(2,1)S(1)} %convolution_convert_fusion.refs_0_), channel_id=1, source_target_pairs={{0,192},{4,196},{8,200},{12,204},{16,208},{20,212},{24,216},{28,22... | collective-permute-start | bytes 49160 | tf_op jit(solution)/shard_map/level5/ppermute | solution.py:18
  42.1 0.3 convolution_add_fusion.4
  42.3 0.3 convolution_add_fusion.3
  42.6 0.3 convolution_add_fusion.2
  42.9 1.1 %collective-permute-done.14 = bf16[32,256]{1,0:T(8,128)(2,1)S(1)} collective-permute-done((bf16[32,256]{1,0:T(8,128)(2,1)S(1)}, bf16[32,256]{1,0:T(8,128)(2,1)S(1)}, u32[]{:S(2)}, u32[]{:S(2)}) %collective-permute-start.14) | collective-permute-done | bytes 16416 | tf_op jit(solution)/shard_map/level5/ppermute | solution.py:18
  44.0 0.3 convolution_add_fusion.1.refs_0_
  44.3 7.6 %collective-permute-start.15 = (f32[32,256]{1,0:T(8,128)S(1)}, f32[32,256]{1,0:T(8,128)S(1)}, u32[]{:S(2)}, u32[]{:S(2)}) collective-permute-start(f32[32,256]{1,0:T(8,128)S(1)} %convolution_add_fusion.1.refs_0_), channel_id=1, source_target_pairs={{0,4},{4,0},{8,12},{12,8},{16,20},{20,16},{24,28},{28,24},{32,36},... | collective-permute-start | bytes 98312 | tf_op jit(solution)/shard_map/down/ppermute | solution.py:18
  51.9 0.9 %collective-permute-done.15 = f32[32,256]{1,0:T(8,128)S(1)} collective-permute-done((f32[32,256]{1,0:T(8,128)S(1)}, f32[32,256]{1,0:T(8,128)S(1)}, u32[]{:S(2)}, u32[]{:S(2)}) %collective-permute-start.15) | collective-permute-done | bytes 32800 | tf_op jit(solution)/shard_map/down/ppermute | solution.py:18
  52.8 0.3 convolution_add_fusion.signal.own
  53.0 0.0 collective-permute-done.10.refs_0_
  53.1 0.0 collective-permute-done.11.refs_1_
  53.1 0.1 collective-permute-start.16
  53.2 1.3 %near.8.refs_2_ = f32[4,512,128]{2,1,0:T(8,128)S(1)} custom-call(s32[1]{0:T(128)} %bitcast.3.place, bf16[4,512,2048]{2,1,0:T(8,128)(2,1)S(1)} %copy-done, f32[64,256]{1,0:T(8,128)S(1)} %convolution_add_fusion.signal.own, bf16[4,512,128]{2,1,0:T(8,128)(2,1)S(1)} %get-tuple-element.51.refs_0_, bf16[4,512,128]{2,1,0:T(8,128)(2,1)S(1)} %get-tuple-element.52.refs_1_, ...), custom_call_target="tpu_custom_call" | custom-call | flops 2147483648 | bytes 4096 | tf_op jit(solution)/shard_map/down/near/pallas_call | solution.py:204
  54.4 0.0 copy-start.2
  54.5 0.0 copy-start.4
  54.5 0.7 %near.10 = f32[4,512,128]{2,1,0:T(8,128)S(1)} custom-call(s32[1]{0:T(128)} %bitcast.3.place, bf16[4,512,2048]{2,1,0:T(8,128)(2,1)S(1)} %copy-done, f32[64,256]{1,0:T(8,128)S(1)} %convolution_add_fusion.signal.own, bf16[2,512,128]{2,1,0:T(8,128)(2,1)S(1)} %collective-permute-done.10.refs_0_, bf16[2,512,128]{2,1,0:T(8,128)(2,1)S(1)} %collective-permute-done.11.refs_1_, ...), custom_call_target="tpu_custom_call" | custom-call | flops 2147483648 | bytes 4096 | tf_op jit(solution)/shard_map/down/near/pallas_call | solution.py:204
  55.2 1.1 %collective-permute-done.16.other = f32[64,256]{1,0:T(8,128)S(1)} collective-permute-done((f32[64,256]{1,0:T(8,128)S(1)}, f32[64,256]{1,0:T(8,128)S(1)}, u32[]{:S(2)}, u32[]{:S(2)}) %collective-permute-start.16) | collective-permute-done | bytes 65568 | tf_op jit(solution)/shard_map/down/ppermute | solution.py:18
  56.3 0.0 copy-done.4
  56.3 1.9 %final.1 = bf16[4,512,128]{2,1,0:T(8,128)(2,1)} custom-call(s32[1]{0:T(128)} %bitcast.half, f32[64,256]{1,0:T(8,128)S(1)} %convolution_add_fusion.signal.own, f32[64,256]{1,0:T(8,128)S(1)} %collective-permute-done.16.other, f32[4,64,256]{2,1,0:T(8,128)S(1)} %down.1.side_own, bf16[4,64,256]{2,1,0:T(8,128)(2,1)S(1)} %collective-permute-done.12.side_other, ...), custom_call_target="tpu_custom_call" | custom-call | flops 134217728 | bytes 4194304 | tf_op jit(solution)/shard_map/final/pallas_call | solution.py:292
  (43 shorter events, 0.3 us)
Async XLA Ops:
  0.0 9.1 %copy-start.7 = (bf16[2,256,256]{2,1,0:T(8,128)(2,1)S(1)}, bf16[2,256,256]{2,1,0:T(8,128)(2,1)}, u32[]{:S(2)}) copy-start(bf16[2,256,256]{2,1,0:T(8,128)(2,1)} %lc.1) | copy-start | bytes 786436
  0.0 9.1 %copy-start.8 = (bf16[1,256,256]{2,1,0:T(8,128)(2,1)S(1)}, bf16[1,256,256]{2,1,0:T(8,128)(2,1)}, u32[]{:S(2)}) copy-start(bf16[1,256,256]{2,1,0:T(8,128)(2,1)} %mc.1) | copy-start | bytes 393220
  0.0 9.1 %copy-start.6 = (bf16[1,5,256,256]{3,2,1,0:T(8,128)(2,1)S(1)}, bf16[1,5,256,256]{3,2,1,0:T(8,128)(2,1)}, u32[]{:S(2)}) copy-start(bf16[1,5,256,256]{3,2,1,0:T(8,128)(2,1)} %ct.1) | copy-start | bytes 1966084
  0.0 9.1 %copy-start.5 = (bf16[1,6,256,256]{3,2,1,0:T(8,128)(2,1)S(1)}, bf16[1,6,256,256]{3,2,1,0:T(8,128)(2,1)}, u32[]{:S(2)}) copy-start(bf16[1,6,256,256]{3,2,1,0:T(8,128)(2,1)} %cc.1) | copy-start | bytes 2359300
  2.5 3.8 %collective-permute-start = (f32[64,256]{1,0:T(8,128)S(1)}, f32[64,256]{1,0:T(8,128)S(1)}, u32[]{:S(2)}, u32[]{:S(2)}) collective-permute-start(f32[64,256]{1,0:T(8,128)S(1)} %get-tuple-element.36), channel_id=1, source_target_pairs={{0,1},{1,0},{2,3},{3,2},{4,5},{5,4},{6,7},{7,6},{8,9},{9,8},{10,11... | collective-permute-start | bytes 196616 | tf_op jit(solution)/shard_map/row_sum/ppermute | solution.py:18
  6.3 13.6 %copy-start.3 = (bf16[4,512,128]{2,1,0:T(8,128)(2,1)S(1)}, bf16[4,512,128]{2,1,0:T(8,128)(2,1)}, u32[]{:S(2)}) copy-start(bf16[4,512,128]{2,1,0:T(8,128)(2,1)} %refs_0_.1) | copy-start | bytes 1572868
  6.3 4.5 %collective-permute-start.1 = (f32[64,256]{1,0:T(8,128)S(1)}, f32[64,256]{1,0:T(8,128)S(1)}, u32[]{:S(2)}, u32[]{:S(2)}) collective-permute-start(f32[64,256]{1,0:T(8,128)S(1)} %add.51.refs_0_), channel_id=1, source_target_pairs={{0,3},{1,2},{2,1},{3,0},{4,7},{5,6},{6,5},{7,4},{8,11},{9,10},{10,... | collective-permute-start | bytes 196616 | tf_op jit(solution)/shard_map/row_sum/ppermute | solution.py:18
  9.1 17.6 %copy-start = (bf16[4,512,2048]{2,1,0:T(8,128)(2,1)S(1)}, bf16[4,512,2048]{2,1,0:T(8,128)(2,1)}, u32[]{:S(2)}) copy-start(bf16[4,512,2048]{2,1,0:T(8,128)(2,1)} %near.11) | copy-start | bytes 25165828
  9.6 6.4 %collective-permute-start.5 = (bf16[4,64,256]{2,1,0:T(8,128)(2,1)S(1)}, bf16[4,64,256]{2,1,0:T(8,128)(2,1)S(1)}, u32[]{:S(2)}, u32[]{:S(2)}) collective-permute-start(bf16[4,64,256]{2,1,0:T(8,128)(2,1)S(1)} %row_sum.1), channel_id=1, source_target_pairs={{0,1},{1,0},{2,3},{3,2},{4,5},{5,4},{6,7},{7,6},{8,9},{9,8},{10,11... | collective-permute-start | bytes 393224 | tf_op jit(solution)/shard_map/row_sum/ppermute | solution.py:18
  11.1 5.9 %collective-permute-start.2 = (f32[96,256]{1,0:T(8,128)S(1)}, f32[96,256]{1,0:T(8,128)S(1)}, u32[]{:S(2)}, u32[]{:S(2)}) collective-permute-start(f32[96,256]{1,0:T(8,128)S(1)} %pad_maximum_fusion.refs_0_), channel_id=1, source_target_pairs={{0,4},{4,0},{8,12},{12,8},{16,20},{20,16},{24,28},{28,24},{32,36},... | collective-permute-start | bytes 294920 | tf_op jit(solution)/shard_map/level0/ppermute | solution.py:18
  17.3 5.3 %collective-permute-start.7 = (bf16[32,768]{1,0:T(8,128)(2,1)S(1)}, bf16[32,768]{1,0:T(8,128)(2,1)S(1)}, u32[]{:S(2)}, u32[]{:S(2)}) collective-permute-start(bf16[32,768]{1,0:T(8,128)(2,1)S(1)} %pad_maximum_fusion.1), channel_id=1, source_target_pairs={{0,8},{4,12},{8,0},{12,4},{16,24},{20,28},{24,16},{28,20},{32,40},... | collective-permute-start | bytes 147464 | tf_op jit(solution)/shard_map/level1/ppermute | solution.py:18
  17.4 5.5 %collective-permute-start.6 = (bf16[4,64,256]{2,1,0:T(8,128)(2,1)S(1)}, bf16[4,64,256]{2,1,0:T(8,128)(2,1)S(1)}, u32[]{:S(2)}, u32[]{:S(2)}) collective-permute-start(bf16[4,64,256]{2,1,0:T(8,128)(2,1)S(1)} %get-tuple-element.65), channel_id=1, source_target_pairs={{0,3},{1,2},{2,1},{3,0},{4,7},{5,6},{6,5},{7,4},{8,11},{9,10},{10,... | collective-permute-start | bytes 393224 | tf_op jit(solution)/shard_map/level0/side2/ppermute | solution.py:18
  19.9 15.2 %collective-permute-start.3 = (bf16[4,512,128]{2,1,0:T(8,128)(2,1)S(1)}, bf16[4,512,128]{2,1,0:T(8,128)(2,1)S(1)}, u32[]{:S(2)}, u32[]{:S(2)}) collective-permute-start(bf16[4,512,128]{2,1,0:T(8,128)(2,1)S(1)} %copy-done.3), channel_id=1, source_target_pairs={{0,1},{1,2},{2,3},{3,0},{4,5},{5,6},{6,7},{7,4},{8,9},{9,10},{10,1... | collective-permute-start | bytes 1572872 | tf_op jit(solution)/shard_map/level1/ring/ppermute | solution.py:23
  19.9 15.2 %collective-permute-start.4 = (bf16[4,512,128]{2,1,0:T(8,128)(2,1)S(1)}, bf16[4,512,128]{2,1,0:T(8,128)(2,1)S(1)}, u32[]{:S(2)}, u32[]{:S(2)}) collective-permute-start(bf16[4,512,128]{2,1,0:T(8,128)(2,1)S(1)} %copy-done.3), channel_id=1, source_target_pairs={{0,3},{1,0},{2,1},{3,2},{4,7},{5,4},{6,5},{7,6},{8,11},{9,8},{10,9... | collective-permute-start | bytes 1572872 | tf_op jit(solution)/shard_map/level1/ring/ppermute | solution.py:23
  22.9 5.6 %collective-permute-start.8 = (bf16[32,768]{1,0:T(8,128)(2,1)S(1)}, bf16[32,768]{1,0:T(8,128)(2,1)S(1)}, u32[]{:S(2)}, u32[]{:S(2)}) collective-permute-start(bf16[32,768]{1,0:T(8,128)(2,1)S(1)} %pad_maximum_fusion.2.signal.refs_0_), channel_id=1, source_target_pairs={{0,16},{4,20},{8,24},{12,28},{16,0},{20,4},{24,8},{28,12},{32,48},... | collective-permute-start | bytes 147464 | tf_op jit(solution)/shard_map/level2/ppermute | solution.py:18
  26.7 1.0 %copy-start.1 = (bf16[4,256,256]{2,1,0:T(8,128)(2,1)S(1)}, bf16[4,256,256]{2,1,0:T(8,128)(2,1)}, u32[]{:S(2)}) copy-start(bf16[4,256,256]{2,1,0:T(8,128)(2,1)} %lt.5) | copy-start | bytes 1572868
  28.8 5.4 %collective-permute-start.9 = (bf16[32,768]{1,0:T(8,128)(2,1)S(1)}, bf16[32,768]{1,0:T(8,128)(2,1)S(1)}, u32[]{:S(2)}, u32[]{:S(2)}) collective-permute-start(bf16[32,768]{1,0:T(8,128)(2,1)S(1)} %pad_maximum_fusion.3.refs_0_), channel_id=1, source_target_pairs={{0,48},{4,52},{8,56},{12,60},{16,32},{20,36},{24,40},{28,44},{32,1... | collective-permute-start | bytes 147464 | tf_op jit(solution)/shard_map/level3/ppermute | solution.py:18
  35.0 4.2 %collective-permute-start.13 = (bf16[32,768]{1,0:T(8,128)(2,1)S(1)}, bf16[32,768]{1,0:T(8,128)(2,1)S(1)}, u32[]{:S(2)}, u32[]{:S(2)}) collective-permute-start(bf16[32,768]{1,0:T(8,128)(2,1)S(1)} %pad_maximum_fusion.4.refs_0_), channel_id=1, source_target_pairs={{0,64},{4,68},{8,72},{12,76},{16,80},{20,84},{24,88},{28,92},{32,9... | collective-permute-start | bytes 147464 | tf_op jit(solution)/shard_map/level4/ppermute | solution.py:18
  36.3 3.8 %collective-permute-start.12 = (bf16[4,64,256]{2,1,0:T(8,128)(2,1)S(1)}, bf16[4,64,256]{2,1,0:T(8,128)(2,1)S(1)}, u32[]{:S(2)}, u32[]{:S(2)}) collective-permute-start(bf16[4,64,256]{2,1,0:T(8,128)(2,1)S(1)} %side3.1), channel_id=1, source_target_pairs={{0,1},{1,0},{2,3},{3,2},{4,5},{5,4},{6,7},{7,6},{8,9},{9,8},{10,11... | collective-permute-start | bytes 393224 | tf_op jit(solution)/shard_map/level3/side3/ppermute | solution.py:18
  36.4 16.7 %collective-permute-start.10 = (bf16[2,512,128]{2,1,0:T(8,128)(2,1)S(1)}, bf16[2,512,128]{2,1,0:T(8,128)(2,1)S(1)}, u32[]{:S(2)}, u32[]{:S(2)}) collective-permute-start(bf16[2,512,128]{2,1,0:T(8,128)(2,1)S(1)} %slice.160), channel_id=1, source_target_pairs={{0,1},{1,2},{2,3},{3,0},{4,5},{5,6},{6,7},{7,4},{8,9},{9,10},{10,1... | collective-permute-start | bytes 786440 | tf_op jit(solution)/shard_map/level4/across/ppermute | solution.py:23
  37.9 15.1 %collective-permute-start.11 = (bf16[2,512,128]{2,1,0:T(8,128)(2,1)S(1)}, bf16[2,512,128]{2,1,0:T(8,128)(2,1)S(1)}, u32[]{:S(2)}, u32[]{:S(2)}) collective-permute-start(bf16[2,512,128]{2,1,0:T(8,128)(2,1)S(1)} %slice.161), channel_id=1, source_target_pairs={{0,3},{1,0},{2,1},{3,2},{4,7},{5,4},{6,5},{7,6},{8,11},{9,8},{10,9... | collective-permute-start | bytes 786440 | tf_op jit(solution)/shard_map/level4/across/ppermute | solution.py:23
  40.1 3.8 %collective-permute-start.14 = (bf16[32,256]{1,0:T(8,128)(2,1)S(1)}, bf16[32,256]{1,0:T(8,128)(2,1)S(1)}, u32[]{:S(2)}, u32[]{:S(2)}) collective-permute-start(bf16[32,256]{1,0:T(8,128)(2,1)S(1)} %convolution_convert_fusion.refs_0_), channel_id=1, source_target_pairs={{0,192},{4,196},{8,200},{12,204},{16,208},{20,212},{24,216},{28,22... | collective-permute-start | bytes 49160 | tf_op jit(solution)/shard_map/level5/ppermute | solution.py:18
  44.3 8.5 %collective-permute-start.15 = (f32[32,256]{1,0:T(8,128)S(1)}, f32[32,256]{1,0:T(8,128)S(1)}, u32[]{:S(2)}, u32[]{:S(2)}) collective-permute-start(f32[32,256]{1,0:T(8,128)S(1)} %convolution_add_fusion.1.refs_0_), channel_id=1, source_target_pairs={{0,4},{4,0},{8,12},{12,8},{16,20},{20,16},{24,28},{28,24},{32,36},... | collective-permute-start | bytes 98312 | tf_op jit(solution)/shard_map/down/ppermute | solution.py:18
  53.1 3.2 %collective-permute-start.16 = (f32[64,256]{1,0:T(8,128)S(1)}, f32[64,256]{1,0:T(8,128)S(1)}, u32[]{:S(2)}, u32[]{:S(2)}) collective-permute-start(f32[64,256]{1,0:T(8,128)S(1)} %convolution_add_fusion.signal.own), channel_id=1, source_target_pairs={{0,1},{1,0},{2,3},{3,2},{4,5},{5,4},{6,7},{7,6},{8,9},{9,8},{10,11... | collective-permute-start | bytes 196616 | tf_op jit(solution)/shard_map/down/ppermute | solution.py:18
  54.4 1.8 %copy-start.2 = (bf16[4,512,256]{2,1,0:T(8,128)(2,1)S(1)}, bf16[4,512,256]{2,1,0:T(8,128)(2,1)}, u32[]{:S(2)}) copy-start(bf16[4,512,256]{2,1,0:T(8,128)(2,1)} %basis.3) | copy-start | bytes 3145732
  54.5 1.8 %copy-start.4 = (bf16[2,256,256]{2,1,0:T(8,128)(2,1)S(1)}, bf16[2,256,256]{2,1,0:T(8,128)(2,1)}, u32[]{:S(2)}) copy-start(bf16[2,256,256]{2,1,0:T(8,128)(2,1)} %mt.3) | copy-start | bytes 786436

commit v2 on v1

--- a/solution.py
+++ b/solution.py
@@ -151,15 +151,12 @@
     )(half, fields, basis, lt, mt)
 
 
-def stage_kernel(keep, ct, cc, lc, mc, joint, crown, lc_out, mc_out, sems):
+def stage_kernel(keep, ct, cc, joint, sems):
     copies = [
-        pltpu.make_async_copy(ct.at[0], joint.at[:, :, pl.ds(0, 256)], sems.at[0]),
         pltpu.make_async_copy(
-            cc.at[0, pl.ds(0, 5)], joint.at[:, :, pl.ds(256, 256)], sems.at[1]
-        ),
-        pltpu.make_async_copy(cc.at[0, 5], crown, sems.at[2]),
-        pltpu.make_async_copy(lc, lc_out, sems.at[3]),
-        pltpu.make_async_copy(mc, mc_out, sems.at[4]),
+            ct.at[0], joint.at[pl.ds(0, 5), :, pl.ds(0, 256)], sems.at[0]
+        ),
+        pltpu.make_async_copy(cc.at[0], joint.at[:, :, pl.ds(256, 256)], sems.at[1]),
     ]
     for copy in copies:
         copy.start()
@@ -167,22 +164,16 @@
         copy.wait()
 
 
-def stage_mats(keep, ct, cc, lc, mc):
-    vmem = pl.BlockSpec(memory_space=pltpu.VMEM)
+def stage_mats(keep, ct, cc):
     return pl.pallas_call(
         stage_kernel,
-        out_shape=(
-            jax.ShapeDtypeStruct((5, 256, 512), bf16),
-            jax.ShapeDtypeStruct((256, 256), bf16),
-            jax.ShapeDtypeStruct((2, 256, 256), bf16),
-            jax.ShapeDtypeStruct((1, 256, 256), bf16),
-        ),
-        in_specs=[pl.BlockSpec(memory_space=pl.ANY)] * 5,
-        out_specs=(vmem,) * 4,
-        scratch_shapes=[pltpu.SemaphoreType.DMA((5,))],
+        out_shape=jax.ShapeDtypeStruct((6, 256, 512), bf16),
+        in_specs=[pl.BlockSpec(memory_space=pl.ANY)] * 3,
+        out_specs=pl.BlockSpec(memory_space=pltpu.VMEM),
+        scratch_shapes=[pltpu.SemaphoreType.DMA((2,))],
         compiler_params=pltpu.CompilerParams(vmem_limit_bytes=16 << 20),
         cost_estimate=pl.CostEstimate(flops=0, bytes_accessed=4 << 20, transcendentals=0),
-    )(keep, ct, cc, lc, mc)
+    )(keep, ct, cc)
 
 
 def near_kernel(offsets, pieces, started, place, near, signal, *refs):
@@ -327,11 +318,19 @@
         half, fields, leaf_basis, leaf_transfer, mid_transfer
     )
     basis, lt, mt = leaf_basis, leaf_transfer, mid_transfer
-    joint, crown, lc, mc = stage_mats(keep, cross_transfer, cross_couple, leaf_couple, mid_couple)
+    joint = stage_mats(keep, cross_transfer, cross_couple)
+    crown = joint[5, :, 256:]
+    with jax.named_scope("path"):
+        path = joint[1, :, :256].astype(f32)
+        for level in (2, 3, 4):
+            path = times(path, joint[level, :, :256])
     with jax.named_scope("row_sum"):
         current = keep + exchange(send, "row", 1)
+        path, current = lax.optimization_barrier((path, current))
         (side_send,) = hold(current, side_send)
         got_side = exchange(side_send, "row", 1)
+        with jax.named_scope("ring0"):
+            from_left = shifted(after(fields, side_send), 1)
         current = current + exchange(current, "row", 3)
 
     with jax.named_scope("level0"):
@@ -340,65 +339,65 @@
         mine = jnp.where(first_core, lifted[:32], lifted[32:])
         other = jnp.where(first_core, lifted[32:], lifted[:32])
         payload = jnp.concatenate([other, both[:, 256:]], axis=0)
+        (mine,) = hold(payload, mine, flops=1 << 32)
+        got = exchange(payload, "leaf", 1)
+        current = mine + got[:32]
+        incoming = [got[32:]]
+
+    def prepare(level, current):
+        both = times(current, joint[level])
+        lifted = both[:, :256]
+        terms = two_terms(lifted)
+        payload = jnp.concatenate([*terms, both[:, 256:].astype(bf16)], axis=1)
+        return lifted, payload
+
+    def rise(level, lifted, payload):
+        got = exchange(payload, "leaf", PARTNERS[level]).astype(f32)
+        incoming.append(got[:, -256:])
+        partner = got[:, :256]
+        if got.shape[1] > 512:
+            partner = partner + got[:, 256:512]
+        return lifted + partner
+
+    with jax.named_scope("level1"):
+        lifted, payload = prepare(1, current)
         with jax.named_scope("side2"):
             (got_side,) = hold(payload, got_side)
             skel = side_keep + got_side.astype(f32)
-            across_side = exchange(skel.astype(bf16), "row", 3)
-        got = exchange(payload, "leaf", 1)
-        current = mine + got[:32]
-        incoming = [got[32:]]
-
-    def prepare(level, current):
-        both = times(current, joint[level])
-        lifted = both[:, :256]
-        payload = jnp.concatenate([*two_terms(lifted), both[:, 256:].astype(bf16)], axis=1)
-        return lifted, payload
-
-    def rise(level, lifted, payload):
-        got = exchange(payload, "leaf", PARTNERS[level]).astype(f32)
-        incoming.append(got[:, 512:])
-        return lifted + (got[:, :256] + got[:, 256:512])
-
-    with jax.named_scope("level1"):
-        lifted, payload = prepare(1, current)
-        with jax.named_scope("ring"):
-            ready = after(fields, payload)
-            from_left = shifted(ready, 1)
-            from_right = shifted(ready, -1)
+            side_send = skel.astype(bf16)
+            across_side = exchange(side_send, "row", 3)
+        with jax.named_scope("ring1"):
+            from_right = shifted(after(fields, payload, side_send), -1)
         current = rise(1, lifted, payload)
     with jax.named_scope("level2"):
         lifted, payload = prepare(2, current)
-        across_side, payload = lax.optimization_barrier((across_side, payload))
         with jax.named_scope("near"):
             near = near_product(place, near_blocks, payload, (0,), (fields,))
-        with jax.named_scope("side"):
-            side, side_send = side_potentials(payload, skel, across_side, lt, lc, mc)
-        with jax.named_scope("path"):
-            (steps,) = hold(payload, joint[1:5, :, :256])
-            path = steps[0].astype(f32)
-            for level in (1, 2, 3):
-                path = times(path, steps[level])
         current = rise(2, lifted, payload)
     with jax.named_scope("level3"):
         lifted, payload = prepare(3, current)
-        near, side, path, payload = lax.optimization_barrier((near, side, path, payload))
+        near, path, payload = lax.optimization_barrier((near, path, payload))
         with jax.named_scope("side3"):
-            (side_send,) = hold(payload, side_send, flops=1 << 32)
+            (across_side,) = hold(payload, across_side, flops=1 << 32)
+            side, side_send = side_potentials(payload, skel, across_side, lt, leaf_couple, mid_couple)
             side_other = exchange(side_send, "row", 1)
         current = rise(3, lifted, payload)
     with jax.named_scope("level4"):
         lifted, payload = prepare(4, current)
-        from_left, from_right, side_send, payload = lax.optimization_barrier(
-            (from_left, from_right, side_send, payload)
-        )
+        side, side_send, payload = lax.optimization_barrier((side, side_send, payload))
+        from_left, payload = lax.optimization_barrier((from_left, payload))
+        (side,) = hold(payload, side, flops=1 << 32)
         with jax.named_scope("across"):
-            from_left, from_right = hold(payload, from_left, from_right)
+            (from_left,) = hold(payload, from_left)
             across0 = shifted(from_left[:2], 1)
+            (from_right,) = hold(payload, from_right)
             across1 = shifted(from_right[2:], -1)
         current = rise(4, lifted, payload)
     with jax.named_scope("level5"):
         payload = times(current, crown).astype(bf16)
-        side_other, payload = lax.optimization_barrier((side_other, payload))
+        side_other, side, from_right, payload = lax.optimization_barrier(
+            (side_other, side, from_right, payload)
+        )
         (tail,) = hold(payload, incoming[4])
         for level in (3, 2, 1):
             tail = times_t(tail, joint[level, :, :256]) + incoming[level]
@@ -412,9 +411,7 @@
         top = jnp.where(first_core, potential, other)
         bottom = jnp.where(first_core, other, potential)
         potential = times_t(jnp.concatenate([top, bottom]), joint[0, :, :256]) + incoming[0]
-        across0, across1, side, potential = lax.optimization_barrier(
-            (across0, across1, side, potential)
-        )
+        side, potential = lax.optimization_barrier((side, potential))
         with jax.named_scope("near"):
             near = near_product(
                 place, near_blocks, potential, (3, 1), (from_left, from_right), near

time: 58.5 us -> 53.3 us (0.911)
  waiting for transfers between devices: 9.43 us -> 6.42 us
  starting transfers between devices: 35.9 us -> 34.4 us
    ppermute x13, waiting for transfers between devices: 8.85 us -> 6.41 us  [exchange(): return lax.ppermute(value, axis, [(i, i ^ mask) for i in range(count)])]
    ppermute x13, starting transfers between devices: 30.3 us -> 28.9 us  [exchange(): return lax.ppermute(value, axis, [(i, i ^ mask) for i in range(count)])]
  transfers between devices with their start and end apart: 17 -> 17, of which waited for: 9 -> 9; matrix products, arithmetic and copies ran while one was open for 6% -> 7% of each run, Pallas kernels for 7% -> 7%
where the time goes in v2:
time: 53.3 us; the launch traced here: 53.2 us
  starting transfers between devices  34.4 us (65%)
  Pallas kernels  7.9 us (15%)
  waiting for transfers between devices  6.42 us (12%)
  matrix products  3.52 us (7%)
  between operations  0.58 us (1%)
    ppermute x13, starting transfers between devices, exchange(): return lax.ppermute(value, axis, [(i, i ^ mask) for i in range(count)])  28.9 us
    ppermute x13, waiting for transfers between devices, exchange(): return lax.ppermute(value, axis, [(i, i ^ mask) for i in range(count)])  6.41 us
    ppermute x4, starting transfers between devices, shifted(): lax.ppermute(value, 'row', [(i, (i + step) % count) for i in range(count)])  5.58 us
    pallas_call x3, Pallas kernels, near_product(): pl.pallas_call(functools.partial(near_kernel, offsets, len(parts), bool(e...  2.7 us
    pallas_call x1, Pallas kernels, gather_skeletons(): pl.pallas_call(gather_kernel, out_shape=(jax.ShapeDtypeStruct((64, 256),...  2.42 us
    dot_general x9, matrix products, times(): lax.dot_general(values, mats.astype(f32), (((1,), (0,)), ((), ())), preci...  2.11 us
    pallas_call x1, Pallas kernels, final_product(): pl.pallas_call(final_kernel, out_shape=jax.ShapeDtypeStruct((4, 512, 128)...  1.93 us
    dot_general x5, matrix products, times_t(): lax.dot_general(values, mats.astype(f32), (((1,), (1,)), ((), ())), preci...  1.41 us
  transfers between devices with their start and end apart: 17, of which 9 were waited for; matrix products, arithmetic and copies ran while one was open for 7% of the time, Pallas kernels for 7%

profile of v2, /device:TPU:1, one launch (start us, length us, event | category | flops | bytes accessed | tf_op | source)
XLA Modules:
  0.0 53.2 jit_solution(3461175400193235498)
XLA Ops:
  0.0 2.4 %shard_map.91 = (f32[64,256]{1,0:T(8,128)S(1)}, f32[64,256]{1,0:T(8,128)S(1)}, f32[4,64,256]{2,1,0:T(8,128)S(1)}, bf16[4,64,256]{2,1,0:T(8,128)(2,1)S(1)}) custom-call(s32[1]{0:T(128)} %bitcast.half, bf16[4,512,128]{2,1,0:T(8,128)(2,1)} %refs_0_.1, bf16[4,512,256]{2,1,0:T(8,128)(2,1)} %basis.3, bf16[4,256,256]{2,1,0:T(8,128)(2,1)} %lt.5, bf16[2,256,256]{2,1,0:T(8,128)(2,1)} %mt.3), custom_call_target="tpu_custom_call" | custom-call | flops 134217728 | bytes 3145728 | tf_op jit(solution)/shard_map/pallas_call | solution.py:129
  2.4 2.1 %collective-permute-start = (f32[64,256]{1,0:T(8,128)S(1)}, f32[64,256]{1,0:T(8,128)S(1)}, u32[]{:S(2)}, u32[]{:S(2)}) collective-permute-start(f32[64,256]{1,0:T(8,128)S(1)} %get-tuple-element.31), channel_id=1, source_target_pairs={{0,1},{1,0},{2,3},{3,2},{4,5},{5,4},{6,7},{7,6},{8,9},{9,8},{10,11... | collective-permute-start | bytes 196616 | tf_op jit(solution)/shard_map/row_sum/ppermute | solution.py:18
  4.6 0.0 copy-done.4
  4.6 0.0 copy-done.5
  4.6 0.1 shard_map.92
  4.7 0.0 copy-start.2
  4.7 0.2 fusion.6
  4.9 0.3 fusion.7
  5.2 0.3 fusion.5
  5.5 0.8 %collective-permute-done = f32[64,256]{1,0:T(8,128)S(1)} collective-permute-done((f32[64,256]{1,0:T(8,128)S(1)}, f32[64,256]{1,0:T(8,128)S(1)}, u32[]{:S(2)}, u32[]{:S(2)}) %collective-permute-start) | collective-permute-done | bytes 65568 | tf_op jit(solution)/shard_map/row_sum/ppermute | solution.py:18
  6.2 2.8 %collective-permute-start.1 = (f32[64,256]{1,0:T(8,128)S(1)}, f32[64,256]{1,0:T(8,128)S(1)}, u32[]{:S(2)}, u32[]{:S(2)}) collective-permute-start(f32[64,256]{1,0:T(8,128)S(1)} %add.51.refs_0_), channel_id=1, source_target_pairs={{0,3},{1,2},{2,1},{3,0},{4,7},{5,6},{6,5},{7,4},{8,11},{9,10},{10,... | collective-permute-start | bytes 196616 | tf_op jit(solution)/shard_map/row_sum/ppermute | solution.py:18
  9.1 0.0 collective-permute-start.5
  9.1 0.0 copy-done.2
  9.1 1.5 %collective-permute-start.8 = (bf16[4,512,128]{2,1,0:T(8,128)(2,1)S(1)}, bf16[4,512,128]{2,1,0:T(8,128)(2,1)S(1)}, u32[]{:S(2)}, u32[]{:S(2)}) collective-permute-start(bf16[4,512,128]{2,1,0:T(8,128)(2,1)S(1)} %copy-done.2), channel_id=1, source_target_pairs={{0,1},{1,2},{2,3},{3,0},{4,5},{5,6},{6,7},{7,4},{8,9},{9,10},{10,1... | collective-permute-start | bytes 1572872 | tf_op jit(solution)/shard_map/row_sum/ring0/ppermute | solution.py:23
  10.5 0.2 collective-permute-done.1
  10.7 0.3 fusion.4
  11.0 5.7 %collective-permute-start.2 = (f32[96,256]{1,0:T(8,128)S(1)}, f32[96,256]{1,0:T(8,128)S(1)}, u32[]{:S(2)}, u32[]{:S(2)}) collective-permute-start(f32[96,256]{1,0:T(8,128)S(1)} %pad_maximum_fusion.refs_0_), channel_id=1, source_target_pairs={{0,4},{4,0},{8,12},{12,8},{16,20},{20,16},{24,28},{28,24},{32,36},... | collective-permute-start | bytes 294920 | tf_op jit(solution)/shard_map/level0/ppermute | solution.py:18
  16.8 0.9 %collective-permute-done.2 = f32[96,256]{1,0:T(8,128)S(1)} collective-permute-done((f32[96,256]{1,0:T(8,128)S(1)}, f32[96,256]{1,0:T(8,128)S(1)}, u32[]{:S(2)}, u32[]{:S(2)}) %collective-permute-start.2) | collective-permute-done | bytes 98336 | tf_op jit(solution)/shard_map/level0/ppermute | solution.py:18
  17.7 0.2 fusion.3
  18.0 0.1 collective-permute-start.3
  18.1 0.0 collective-permute-done.5.refs_1_
  18.2 1.7 %collective-permute-start.6 = (bf16[4,64,256]{2,1,0:T(8,128)(2,1)S(1)}, bf16[4,64,256]{2,1,0:T(8,128)(2,1)S(1)}, u32[]{:S(2)}, u32[]{:S(2)}) collective-permute-start(bf16[4,64,256]{2,1,0:T(8,128)(2,1)S(1)} %get-tuple-element.55), channel_id=1, source_target_pairs={{0,3},{1,2},{2,1},{3,0},{4,7},{5,6},{6,5},{7,4},{8,11},{9,10},{10,... | collective-permute-start | bytes 393224 | tf_op jit(solution)/shard_map/level1/side2/ppermute | solution.py:18
  19.8 1.1 %collective-permute-start.10 = (bf16[4,512,128]{2,1,0:T(8,128)(2,1)S(1)}, bf16[4,512,128]{2,1,0:T(8,128)(2,1)S(1)}, u32[]{:S(2)}, u32[]{:S(2)}) collective-permute-start(bf16[4,512,128]{2,1,0:T(8,128)(2,1)S(1)} %copy-done.2), channel_id=1, source_target_pairs={{0,3},{1,0},{2,1},{3,2},{4,7},{5,4},{6,5},{7,6},{8,11},{9,8},{10,9... | collective-permute-start | bytes 1572872 | tf_op jit(solution)/shard_map/level1/ring1/ppermute | solution.py:23
  20.9 0.4 collective-permute-done.3
  21.3 0.2 fusion.2
  21.6 2.3 %collective-permute-start.4 = (bf16[32,768]{1,0:T(8,128)(2,1)S(1)}, bf16[32,768]{1,0:T(8,128)(2,1)S(1)}, u32[]{:S(2)}, u32[]{:S(2)}) collective-permute-start(bf16[32,768]{1,0:T(8,128)(2,1)S(1)} %pad_maximum_fusion.2.signal), channel_id=1, source_target_pairs={{0,16},{4,20},{8,24},{12,28},{16,0},{20,4},{24,8},{28,12},{32,48},... | collective-permute-start | bytes 147464 | tf_op jit(solution)/shard_map/level2/ppermute | solution.py:18
  23.9 0.7 %near.6.refs_2_ = f32[4,512,128]{2,1,0:T(8,128)S(1)} custom-call(s32[1]{0:T(128)} %bitcast.1.place, bf16[4,512,2048]{2,1,0:T(8,128)(2,1)S(1)} %bitcast.46, bf16[32,768]{1,0:T(8,128)(2,1)S(1)} %pad_maximum_fusion.2.signal, bf16[4,512,128]{2,1,0:T(8,128)(2,1)S(1)} %copy-done.2), custom_call_target="tpu_custom_call" | custom-call | flops 2147483648 | bytes 4096 | tf_op jit(solution)/shard_map/level2/near/pallas_call | solution.py:195
  24.6 1.2 %collective-permute-done.4 = bf16[32,768]{1,0:T(8,128)(2,1)S(1)} collective-permute-done((bf16[32,768]{1,0:T(8,128)(2,1)S(1)}, bf16[32,768]{1,0:T(8,128)(2,1)S(1)}, u32[]{:S(2)}, u32[]{:S(2)}) %collective-permute-start.4) | collective-permute-done | bytes 49184 | tf_op jit(solution)/shard_map/level2/ppermute | solution.py:18
  25.9 0.2 fusion.1
  26.1 0.0 copy-start
  26.2 0.0 copy-start.6
  26.2 0.0 copy-start.7
  26.2 4.4 %collective-permute-start.9 = (bf16[32,768]{1,0:T(8,128)(2,1)S(1)}, bf16[32,768]{1,0:T(8,128)(2,1)S(1)}, u32[]{:S(2)}, u32[]{:S(2)}) collective-permute-start(bf16[32,768]{1,0:T(8,128)(2,1)S(1)} %pad_maximum_fusion.3.refs_0_.signal), channel_id=1, source_target_pairs={{0,48},{4,52},{8,56},{12,60},{16,32},{20,36},{24,40},{28,44},{32,1... | collective-permute-start | bytes 147464 | tf_op jit(solution)/shard_map/level3/ppermute | solution.py:18
  30.6 0.0 collective-permute-done.6.refs_1_
  30.6 0.7 %side3.3 = (f32[4,64,256]{2,1,0:T(8,128)S(1)}, bf16[4,64,256]{2,1,0:T(8,128)(2,1)S(1)}) custom-call(bf16[32,768]{1,0:T(8,128)(2,1)S(1)} %pad_maximum_fusion.3.refs_0_.signal, f32[4,64,256]{2,1,0:T(8,128)S(1)} %get-tuple-element.56.own, bf16[4,64,256]{2,1,0:T(8,128)(2,1)S(1)} %side3.2.got, bf16[4,256,256]{2,1,0:T(8,128)(2,1)S(1)} %copy-done, ...), custom_call_target="tpu_custom_call" | custom-call | flops 16777216 | bytes 4096 | tf_op jit(solution)/shard_map/level3/side3/pallas_call | solution.py:228
  31.3 0.6 %collective-permute-start.7 = (bf16[4,64,256]{2,1,0:T(8,128)(2,1)S(1)}, bf16[4,64,256]{2,1,0:T(8,128)(2,1)S(1)}, u32[]{:S(2)}, u32[]{:S(2)}) collective-permute-start(bf16[4,64,256]{2,1,0:T(8,128)(2,1)S(1)} %get-tuple-element.37), channel_id=1, source_target_pairs={{0,1},{1,0},{2,3},{3,2},{4,5},{5,4},{6,7},{7,6},{8,9},{9,8},{10,11... | collective-permute-start | bytes 393224 | tf_op jit(solution)/shard_map/level3/side3/ppermute | solution.py:18
  32.0 0.2 collective-permute-done.9
  32.2 0.2 fusion
  32.5 0.0 collective-permute-done.8.refs_1_
  32.5 1.4 %collective-permute-start.11 = (bf16[32,768]{1,0:T(8,128)(2,1)S(1)}, bf16[32,768]{1,0:T(8,128)(2,1)S(1)}, u32[]{:S(2)}, u32[]{:S(2)}) collective-permute-start(bf16[32,768]{1,0:T(8,128)(2,1)S(1)} %pad_maximum_fusion.4.refs_0_), channel_id=1, source_target_pairs={{0,64},{4,68},{8,72},{12,76},{16,80},{20,84},{24,88},{28,92},{32,9... | collective-permute-start | bytes 147464 | tf_op jit(solution)/shard_map/level4/ppermute | solution.py:18
  33.9 0.8 %collective-permute-start.15 = (bf16[2,512,128]{2,1,0:T(8,128)(2,1)S(1)}, bf16[2,512,128]{2,1,0:T(8,128)(2,1)S(1)}, u32[]{:S(2)}, u32[]{:S(2)}) collective-permute-start(bf16[2,512,128]{2,1,0:T(8,128)(2,1)S(1)} %slice.200), channel_id=1, source_target_pairs={{0,1},{1,2},{2,3},{3,0},{4,5},{5,6},{6,7},{7,4},{8,9},{9,10},{10,1... | collective-permute-start | bytes 786440 | tf_op jit(solution)/shard_map/level4/across/ppermute | solution.py:23
  34.7 0.8 %collective-permute-done.11 = bf16[32,768]{1,0:T(8,128)(2,1)S(1)} collective-permute-done((bf16[32,768]{1,0:T(8,128)(2,1)S(1)}, bf16[32,768]{1,0:T(8,128)(2,1)S(1)}, u32[]{:S(2)}, u32[]{:S(2)}) %collective-permute-start.11) | collective-permute-done | bytes 49184 | tf_op jit(solution)/shard_map/level4/ppermute | solution.py:18
  35.5 0.2 convolution_convert_fusion.refs_0_
  35.7 0.0 collective-permute-done.10.refs_1_
  35.7 0.0 collective-permute-done.7.side_other
  35.8 2.8 %collective-permute-start.12 = (bf16[32,256]{1,0:T(8,128)(2,1)S(1)}, bf16[32,256]{1,0:T(8,128)(2,1)S(1)}, u32[]{:S(2)}, u32[]{:S(2)}) collective-permute-start(bf16[32,256]{1,0:T(8,128)(2,1)S(1)} %convolution_convert_fusion.refs_0_), channel_id=1, source_target_pairs={{0,192},{4,196},{8,200},{12,204},{16,208},{20,212},{24,216},{28,22... | collective-permute-start | bytes 49160 | tf_op jit(solution)/shard_map/level5/ppermute | solution.py:18
  38.6 0.3 convolution_add_fusion.4
  38.8 0.3 convolution_add_fusion.3
  39.1 0.3 convolution_add_fusion.2
  39.4 2.2 %collective-permute-start.16 = (bf16[2,512,128]{2,1,0:T(8,128)(2,1)S(1)}, bf16[2,512,128]{2,1,0:T(8,128)(2,1)S(1)}, u32[]{:S(2)}, u32[]{:S(2)}) collective-permute-start(bf16[2,512,128]{2,1,0:T(8,128)(2,1)S(1)} %slice.201), channel_id=1, source_target_pairs={{0,3},{1,0},{2,1},{3,2},{4,7},{5,4},{6,5},{7,6},{8,11},{9,8},{10,9... | collective-permute-start | bytes 786440 | tf_op jit(solution)/shard_map/level4/across/ppermute | solution.py:23
  41.6 0.0 collective-permute-done.12
  41.6 0.3 convolution_add_fusion.1.refs_0_
  42.0 4.7 %collective-permute-start.13 = (f32[32,256]{1,0:T(8,128)S(1)}, f32[32,256]{1,0:T(8,128)S(1)}, u32[]{:S(2)}, u32[]{:S(2)}) collective-permute-start(f32[32,256]{1,0:T(8,128)S(1)} %convolution_add_fusion.1.refs_0_), channel_id=1, source_target_pairs={{0,4},{4,0},{8,12},{12,8},{16,20},{20,16},{24,28},{28,24},{32,36},... | collective-permute-start | bytes 98312 | tf_op jit(solution)/shard_map/down/ppermute | solution.py:18
  46.7 0.9 %collective-permute-done.13 = f32[32,256]{1,0:T(8,128)S(1)} collective-permute-done((f32[32,256]{1,0:T(8,128)S(1)}, f32[32,256]{1,0:T(8,128)S(1)}, u32[]{:S(2)}, u32[]{:S(2)}) %collective-permute-start.13) | collective-permute-done | bytes 32800 | tf_op jit(solution)/shard_map/down/ppermute | solution.py:18
  47.6 0.3 convolution_add_fusion.signal.own
  47.9 0.1 collective-permute-start.14
  48.0 1.3 %near.8.refs_2_ = f32[4,512,128]{2,1,0:T(8,128)S(1)} custom-call(s32[1]{0:T(128)} %bitcast.1.place, bf16[4,512,2048]{2,1,0:T(8,128)(2,1)S(1)} %bitcast.46, f32[64,256]{1,0:T(8,128)S(1)} %convolution_add_fusion.signal.own, bf16[4,512,128]{2,1,0:T(8,128)(2,1)S(1)} %across.3.refs_0_, bf16[4,512,128]{2,1,0:T(8,128)(2,1)S(1)} %across.2.refs_1_, ...), custom_call_target="tpu_custom_call" | custom-call | flops 2147483648 | bytes 4096 | tf_op jit(solution)/shard_map/down/near/pallas_call | solution.py:195
  49.3 0.0 copy-start.1
  49.3 0.0 copy-start.3
  49.3 0.0 collective-permute-done.15.refs_0_
  49.3 0.0 collective-permute-done.16.refs_1_
  49.3 0.7 %near.10 = f32[4,512,128]{2,1,0:T(8,128)S(1)} custom-call(s32[1]{0:T(128)} %bitcast.1.place, bf16[4,512,2048]{2,1,0:T(8,128)(2,1)S(1)} %bitcast.46, f32[64,256]{1,0:T(8,128)S(1)} %convolution_add_fusion.signal.own, bf16[2,512,128]{2,1,0:T(8,128)(2,1)S(1)} %collective-permute-done.15.refs_0_, bf16[2,512,128]{2,1,0:T(8,128)(2,1)S(1)} %collective-permute-done.16.refs_1_, ...), custom_call_target="tpu_custom_call" | custom-call | flops 2147483648 | bytes 4096 | tf_op jit(solution)/shard_map/down/near/pallas_call | solution.py:195
  50.0 1.1 %collective-permute-done.14.other = f32[64,256]{1,0:T(8,128)S(1)} collective-permute-done((f32[64,256]{1,0:T(8,128)S(1)}, f32[64,256]{1,0:T(8,128)S(1)}, u32[]{:S(2)}, u32[]{:S(2)}) %collective-permute-start.14) | collective-permute-done | bytes 65568 | tf_op jit(solution)/shard_map/down/ppermute | solution.py:18
  51.1 1.9 %final.1 = bf16[4,512,128]{2,1,0:T(8,128)(2,1)} custom-call(s32[1]{0:T(128)} %bitcast.half, f32[64,256]{1,0:T(8,128)S(1)} %convolution_add_fusion.signal.own, f32[64,256]{1,0:T(8,128)S(1)} %collective-permute-done.14.other, f32[4,64,256]{2,1,0:T(8,128)S(1)} %down.1.side_own, bf16[4,64,256]{2,1,0:T(8,128)(2,1)S(1)} %collective-permute-done.7.side_other, ...), custom_call_target="tpu_custom_call" | custom-call | flops 134217728 | bytes 4194304 | tf_op jit(solution)/shard_map/final/pallas_call | solution.py:283
  (47 shorter events, 0.3 us)
Async XLA Ops:
  0.0 4.6 %copy-start.4 = (bf16[1,6,256,256]{3,2,1,0:T(8,128)(2,1)S(1)}, bf16[1,6,256,256]{3,2,1,0:T(8,128)(2,1)}, u32[]{:S(2)}) copy-start(bf16[1,6,256,256]{3,2,1,0:T(8,128)(2,1)} %cc.1) | copy-start | bytes 2359300
  0.0 4.6 %copy-start.5 = (bf16[1,5,256,256]{3,2,1,0:T(8,128)(2,1)S(1)}, bf16[1,5,256,256]{3,2,1,0:T(8,128)(2,1)}, u32[]{:S(2)}) copy-start(bf16[1,5,256,256]{3,2,1,0:T(8,128)(2,1)} %ct.1) | copy-start | bytes 1966084
  2.4 3.8 %collective-permute-start = (f32[64,256]{1,0:T(8,128)S(1)}, f32[64,256]{1,0:T(8,128)S(1)}, u32[]{:S(2)}, u32[]{:S(2)}) collective-permute-start(f32[64,256]{1,0:T(8,128)S(1)} %get-tuple-element.31), channel_id=1, source_target_pairs={{0,1},{1,0},{2,3},{3,2},{4,5},{5,4},{6,7},{7,6},{8,9},{9,8},{10,11... | collective-permute-start | bytes 196616 | tf_op jit(solution)/shard_map/row_sum/ppermute | solution.py:18
  4.7 4.3 %copy-start.2 = (bf16[4,512,128]{2,1,0:T(8,128)(2,1)S(1)}, bf16[4,512,128]{2,1,0:T(8,128)(2,1)}, u32[]{:S(2)}) copy-start(bf16[4,512,128]{2,1,0:T(8,128)(2,1)} %refs_0_.1) | copy-start | bytes 1572868
  6.2 4.5 %collective-permute-start.1 = (f32[64,256]{1,0:T(8,128)S(1)}, f32[64,256]{1,0:T(8,128)S(1)}, u32[]{:S(2)}, u32[]{:S(2)}) collective-permute-start(f32[64,256]{1,0:T(8,128)S(1)} %add.51.refs_0_), channel_id=1, source_target_pairs={{0,3},{1,2},{2,1},{3,0},{4,7},{5,6},{6,5},{7,4},{8,11},{9,10},{10,... | collective-permute-start | bytes 196616 | tf_op jit(solution)/shard_map/row_sum/ppermute | solution.py:18
  9.1 9.0 %collective-permute-start.5 = (bf16[4,64,256]{2,1,0:T(8,128)(2,1)S(1)}, bf16[4,64,256]{2,1,0:T(8,128)(2,1)S(1)}, u32[]{:S(2)}, u32[]{:S(2)}) collective-permute-start(bf16[4,64,256]{2,1,0:T(8,128)(2,1)S(1)} %row_sum.1), channel_id=1, source_target_pairs={{0,1},{1,0},{2,3},{3,2},{4,5},{5,4},{6,7},{7,6},{8,9},{9,8},{10,11... | collective-permute-start | bytes 393224 | tf_op jit(solution)/shard_map/row_sum/ppermute | solution.py:18
  9.1 23.4 %collective-permute-start.8 = (bf16[4,512,128]{2,1,0:T(8,128)(2,1)S(1)}, bf16[4,512,128]{2,1,0:T(8,128)(2,1)S(1)}, u32[]{:S(2)}, u32[]{:S(2)}) collective-permute-start(bf16[4,512,128]{2,1,0:T(8,128)(2,1)S(1)} %copy-done.2), channel_id=1, source_target_pairs={{0,1},{1,2},{2,3},{3,0},{4,5},{5,6},{6,7},{7,4},{8,9},{9,10},{10,1... | collective-permute-start | bytes 1572872 | tf_op jit(solution)/shard_map/row_sum/ring0/ppermute | solution.py:23
  11.0 6.7 %collective-permute-start.2 = (f32[96,256]{1,0:T(8,128)S(1)}, f32[96,256]{1,0:T(8,128)S(1)}, u32[]{:S(2)}, u32[]{:S(2)}) collective-permute-start(f32[96,256]{1,0:T(8,128)S(1)} %pad_maximum_fusion.refs_0_), channel_id=1, source_target_pairs={{0,4},{4,0},{8,12},{12,8},{16,20},{20,16},{24,28},{28,24},{32,36},... | collective-permute-start | bytes 294920 | tf_op jit(solution)/shard_map/level0/ppermute | solution.py:18
  16.8 7.1 %slice-start = ((s8[8388608]{0:T(1024)(128)(4,1)}), s8[4194304]{0:T(1024)(128)(4,1)S(1)}, s32[]{:S(2)}) async-start(s8[8388608]{0:T(1024)(128)(4,1)} %bitcast.45), calls=%async_computation | async-start | bytes 8388608
  16.8 7.1 %slice-start.1 = ((s8[8388608]{0:T(1024)(128)(4,1)}), s8[4194304]{0:T(1024)(128)(4,1)S(1)}, s32[]{:S(2)}) async-start(s8[8388608]{0:T(1024)(128)(4,1)} %bitcast.45), calls=%async_computation.1 | async-start | bytes 8388608
  18.0 3.3 %collective-permute-start.3 = (bf16[32,768]{1,0:T(8,128)(2,1)S(1)}, bf16[32,768]{1,0:T(8,128)(2,1)S(1)}, u32[]{:S(2)}, u32[]{:S(2)}) collective-permute-start(bf16[32,768]{1,0:T(8,128)(2,1)S(1)} %pad_maximum_fusion.1.refs_0_), channel_id=1, source_target_pairs={{0,8},{4,12},{8,0},{12,4},{16,24},{20,28},{24,16},{28,20},{32,40},... | collective-permute-start | bytes 147464 | tf_op jit(solution)/shard_map/level1/ppermute | solution.py:18
  18.2 12.4 %collective-permute-start.6 = (bf16[4,64,256]{2,1,0:T(8,128)(2,1)S(1)}, bf16[4,64,256]{2,1,0:T(8,128)(2,1)S(1)}, u32[]{:S(2)}, u32[]{:S(2)}) collective-permute-start(bf16[4,64,256]{2,1,0:T(8,128)(2,1)S(1)} %get-tuple-element.55), channel_id=1, source_target_pairs={{0,3},{1,2},{2,1},{3,0},{4,7},{5,6},{6,5},{7,4},{8,11},{9,10},{10,... | collective-permute-start | bytes 393224 | tf_op jit(solution)/shard_map/level1/side2/ppermute | solution.py:18
  19.8 15.9 %collective-permute-start.10 = (bf16[4,512,128]{2,1,0:T(8,128)(2,1)S(1)}, bf16[4,512,128]{2,1,0:T(8,128)(2,1)S(1)}, u32[]{:S(2)}, u32[]{:S(2)}) collective-permute-start(bf16[4,512,128]{2,1,0:T(8,128)(2,1)S(1)} %copy-done.2), channel_id=1, source_target_pairs={{0,3},{1,0},{2,1},{3,2},{4,7},{5,4},{6,5},{7,6},{8,11},{9,8},{10,9... | collective-permute-start | bytes 1572872 | tf_op jit(solution)/shard_map/level1/ring1/ppermute | solution.py:23
  21.6 4.2 %collective-permute-start.4 = (bf16[32,768]{1,0:T(8,128)(2,1)S(1)}, bf16[32,768]{1,0:T(8,128)(2,1)S(1)}, u32[]{:S(2)}, u32[]{:S(2)}) collective-permute-start(bf16[32,768]{1,0:T(8,128)(2,1)S(1)} %pad_maximum_fusion.2.signal), channel_id=1, source_target_pairs={{0,16},{4,20},{8,24},{12,28},{16,0},{20,4},{24,8},{28,12},{32,48},... | collective-permute-start | bytes 147464 | tf_op jit(solution)/shard_map/level2/ppermute | solution.py:18
  26.1 4.5 %copy-start = (bf16[4,256,256]{2,1,0:T(8,128)(2,1)S(1)}, bf16[4,256,256]{2,1,0:T(8,128)(2,1)}, u32[]{:S(2)}) copy-start(bf16[4,256,256]{2,1,0:T(8,128)(2,1)} %lt.5) | copy-start | bytes 1572868
  26.2 4.5 %copy-start.6 = (bf16[2,256,256]{2,1,0:T(8,128)(2,1)S(1)}, bf16[2,256,256]{2,1,0:T(8,128)(2,1)}, u32[]{:S(2)}) copy-start(bf16[2,256,256]{2,1,0:T(8,128)(2,1)} %lc.1) | copy-start | bytes 786436
  26.2 4.4 %copy-start.7 = (bf16[1,256,256]{2,1,0:T(8,128)(2,1)S(1)}, bf16[1,256,256]{2,1,0:T(8,128)(2,1)}, u32[]{:S(2)}) copy-start(bf16[1,256,256]{2,1,0:T(8,128)(2,1)} %mc.1) | copy-start | bytes 393220
  26.2 6.0 %collective-permute-start.9 = (bf16[32,768]{1,0:T(8,128)(2,1)S(1)}, bf16[32,768]{1,0:T(8,128)(2,1)S(1)}, u32[]{:S(2)}, u32[]{:S(2)}) collective-permute-start(bf16[32,768]{1,0:T(8,128)(2,1)S(1)} %pad_maximum_fusion.3.refs_0_.signal), channel_id=1, source_target_pairs={{0,48},{4,52},{8,56},{12,60},{16,32},{20,36},{24,40},{28,44},{32,1... | collective-permute-start | bytes 147464 | tf_op jit(solution)/shard_map/level3/ppermute | solution.py:18
  31.3 4.4 %collective-permute-start.7 = (bf16[4,64,256]{2,1,0:T(8,128)(2,1)S(1)}, bf16[4,64,256]{2,1,0:T(8,128)(2,1)S(1)}, u32[]{:S(2)}, u32[]{:S(2)}) collective-permute-start(bf16[4,64,256]{2,1,0:T(8,128)(2,1)S(1)} %get-tuple-element.37), channel_id=1, source_target_pairs={{0,1},{1,0},{2,3},{3,2},{4,5},{5,4},{6,7},{7,6},{8,9},{9,8},{10,11... | collective-permute-start | bytes 393224 | tf_op jit(solution)/shard_map/level3/side3/ppermute | solution.py:18
  32.5 3.0 %collective-permute-start.11 = (bf16[32,768]{1,0:T(8,128)(2,1)S(1)}, bf16[32,768]{1,0:T(8,128)(2,1)S(1)}, u32[]{:S(2)}, u32[]{:S(2)}) collective-permute-start(bf16[32,768]{1,0:T(8,128)(2,1)S(1)} %pad_maximum_fusion.4.refs_0_), channel_id=1, source_target_pairs={{0,64},{4,68},{8,72},{12,76},{16,80},{20,84},{24,88},{28,92},{32,9... | collective-permute-start | bytes 147464 | tf_op jit(solution)/shard_map/level4/ppermute | solution.py:18
  33.9 15.4 %collective-permute-start.15 = (bf16[2,512,128]{2,1,0:T(8,128)(2,1)S(1)}, bf16[2,512,128]{2,1,0:T(8,128)(2,1)S(1)}, u32[]{:S(2)}, u32[]{:S(2)}) collective-permute-start(bf16[2,512,128]{2,1,0:T(8,128)(2,1)S(1)} %slice.200), channel_id=1, source_target_pairs={{0,1},{1,2},{2,3},{3,0},{4,5},{5,6},{6,7},{7,4},{8,9},{9,10},{10,1... | collective-permute-start | bytes 786440 | tf_op jit(solution)/shard_map/level4/across/ppermute | solution.py:23
  35.8 5.9 %collective-permute-start.12 = (bf16[32,256]{1,0:T(8,128)(2,1)S(1)}, bf16[32,256]{1,0:T(8,128)(2,1)S(1)}, u32[]{:S(2)}, u32[]{:S(2)}) collective-permute-start(bf16[32,256]{1,0:T(8,128)(2,1)S(1)} %convolution_convert_fusion.refs_0_), channel_id=1, source_target_pairs={{0,192},{4,196},{8,200},{12,204},{16,208},{20,212},{24,216},{28,22... | collective-permute-start | bytes 49160 | tf_op jit(solution)/shard_map/level5/ppermute | solution.py:18
  39.4 9.9 %collective-permute-start.16 = (bf16[2,512,128]{2,1,0:T(8,128)(2,1)S(1)}, bf16[2,512,128]{2,1,0:T(8,128)(2,1)S(1)}, u32[]{:S(2)}, u32[]{:S(2)}) collective-permute-start(bf16[2,512,128]{2,1,0:T(8,128)(2,1)S(1)} %slice.201), channel_id=1, source_target_pairs={{0,3},{1,0},{2,1},{3,2},{4,7},{5,4},{6,5},{7,6},{8,11},{9,8},{10,9... | collective-permute-start | bytes 786440 | tf_op jit(solution)/shard_map/level4/across/ppermute | solution.py:23
  42.0 5.6 %collective-permute-start.13 = (f32[32,256]{1,0:T(8,128)S(1)}, f32[32,256]{1,0:T(8,128)S(1)}, u32[]{:S(2)}, u32[]{:S(2)}) collective-permute-start(f32[32,256]{1,0:T(8,128)S(1)} %convolution_add_fusion.1.refs_0_), channel_id=1, source_target_pairs={{0,4},{4,0},{8,12},{12,8},{16,20},{20,16},{24,28},{28,24},{32,36},... | collective-permute-start | bytes 98312 | tf_op jit(solution)/shard_map/down/ppermute | solution.py:18
  47.9 3.2 %collective-permute-start.14 = (f32[64,256]{1,0:T(8,128)S(1)}, f32[64,256]{1,0:T(8,128)S(1)}, u32[]{:S(2)}, u32[]{:S(2)}) collective-permute-start(f32[64,256]{1,0:T(8,128)S(1)} %convolution_add_fusion.signal.own), channel_id=1, source_target_pairs={{0,1},{1,0},{2,3},{3,2},{4,5},{5,4},{6,7},{7,6},{8,9},{9,8},{10,11... | collective-permute-start | bytes 196616 | tf_op jit(solution)/shard_map/down/ppermute | solution.py:18
  49.3 1.8 %copy-start.1 = (bf16[4,512,256]{2,1,0:T(8,128)(2,1)S(1)}, bf16[4,512,256]{2,1,0:T(8,128)(2,1)}, u32[]{:S(2)}) copy-start(bf16[4,512,256]{2,1,0:T(8,128)(2,1)} %basis.3) | copy-start | bytes 3145732
  49.3 1.8 %copy-start.3 = (bf16[2,256,256]{2,1,0:T(8,128)(2,1)S(1)}, bf16[2,256,256]{2,1,0:T(8,128)(2,1)}, u32[]{:S(2)}) copy-start(bf16[2,256,256]{2,1,0:T(8,128)(2,1)} %mt.3) | copy-start | bytes 786436

commit v3 on v2

--- a/solution.py
+++ b/solution.py
@@ -88,34 +88,33 @@
     sems,
 ):
     f_copy = pltpu.make_async_copy(fields, f_buf, sems.at[0])
+    lt_copy = pltpu.make_async_copy(lt, lt_out, sems.at[1])
+    mt_copy = pltpu.make_async_copy(mt, mt_out, sems.at[2])
     b_copies = [
-        pltpu.make_async_copy(
-            basis.at[pl.ds(2 * pair, 2)], basis_out.at[pl.ds(2 * pair, 2)], sems.at[1 + pair]
-        )
-        for pair in range(2)
+        pltpu.make_async_copy(basis.at[n], basis_out.at[n], sems.at[3 + n]) for n in range(4)
     ]
-    lt_copy = pltpu.make_async_copy(lt, lt_out, sems.at[3])
-    mt_copy = pltpu.make_async_copy(mt, mt_out, sems.at[4])
-    for copy in (f_copy, *b_copies, lt_copy, mt_copy):
+    for copy in (f_copy, b_copies[0], lt_copy, *b_copies[1:3], mt_copy, b_copies[3]):
         copy.start()
     mine = pl.ds(pl.multiple_of(half[0] * 64, 64), 64)
     other = pl.ds(pl.multiple_of(64 - half[0] * 64, 64), 64)
     f_copy.wait()
-    for n in range(4):
-        if n % 2 == 0:
-            b_copies[n // 2].wait()
-        scratch[n] = lax.dot_general(
+    current = None
+    mid = None
+    for n in range(4):
+        b_copies[n].wait()
+        skel = lax.dot_general(
             f_buf[n], basis_out[n], (((0,), (0,)), ((), ())), preferred_element_type=f32
         )
-    lt_copy.wait()
-    mt_copy.wait()
-    current = None
-    for pair in range(2):
-        mid = split_dot(scratch[2 * pair], lt_out[2 * pair], 0) + split_dot(
-            scratch[2 * pair + 1], lt_out[2 * pair + 1], 0
-        )
-        lifted = split_dot(mid, mt_out[pair], 0)
-        current = lifted if current is None else current + lifted
+        scratch[n] = skel
+        if n == 0:
+            lt_copy.wait()
+        lifted = split_dot(skel, lt_out[n], 0)
+        mid = lifted if n % 2 == 0 else mid + lifted
+        if n == 1:
+            mt_copy.wait()
+        if n % 2:
+            lifted = split_dot(mid, mt_out[n // 2], 0)
+            current = lifted if current is None else current + lifted
     scratch[4] = current
     keep[...] = scratch[4, mine, :]
     send[...] = scratch[4, other, :]
@@ -142,7 +141,7 @@
             pltpu.VMEM((4, 256, 256), bf16),
             pltpu.VMEM((2, 256, 256), bf16),
             pltpu.VMEM((5, 128, 256), f32),
-            pltpu.SemaphoreType.DMA((5,)),
+            pltpu.SemaphoreType.DMA((7,)),
         ],
         compiler_params=pltpu.CompilerParams(vmem_limit_bytes=54528 << 10),
         cost_estimate=pl.CostEstimate(
@@ -262,18 +261,16 @@
     for n in range(4):
         side[n, mine, :] = side_own[n]
         side[n, rest, :] = side_other[n].astype(f32)
+    mids = [split_dot(pot[...], mt[pair], 1) for pair in range(2)]
+    lows = [(split_dot(mids[n // 2], lt[n], 1) + side[n]).astype(bf16) for n in range(4)]
     copies = []
-    for pair in range(2):
-        mid = split_dot(pot[...], mt[pair], 1)
-        for k in range(2):
-            n = 2 * pair + k
-            low = (split_dot(mid, lt[n], 1) + side[n]).astype(bf16)
-            far = lax.dot_general(
-                basis[n], low, (((1,), (1,)), ((), ())), preferred_element_type=f32
-            )
-            buf[n] = (near[n] + far).astype(bf16)
-            copies.append(pltpu.make_async_copy(buf.at[n], out.at[n], sems.at[n]))
-            copies[n].start()
+    for n in range(4):
+        far = lax.dot_general(
+            basis[n], lows[n], (((1,), (1,)), ((), ())), preferred_element_type=f32
+        )
+        buf[n] = (near[n] + far).astype(bf16)
+        copies.append(pltpu.make_async_copy(buf.at[n], out.at[n], sems.at[n]))
+        copies[n].start()
     for copy in copies:
         copy.wait()
 
@@ -347,7 +344,7 @@
     def prepare(level, current):
         both = times(current, joint[level])
         lifted = both[:, :256]
-        terms = two_terms(lifted)
+        terms = two_terms(lifted)[: 1 if level in (4,) else 2]
         payload = jnp.concatenate([*terms, both[:, 256:].astype(bf16)], axis=1)
         return lifted, payload
 

time: 53.3 us -> 53.6 us (level)
    pallas_call x1, Pallas kernels: 2.42 us -> 3.09 us  [gather_skeletons(): pl.pallas_call(gather_kernel, out_shape=(jax.ShapeDtypeStruct((64, 256),...]
where the time goes in v3:
time: 53.6 us; the launch traced here: 53.5 us
  starting transfers between devices  34.6 us (65%)
  Pallas kernels  8.22 us (15%)
  waiting for transfers between devices  6.24 us (12%)
  matrix products  3.52 us (7%)
  between operations  0.58 us (1%)
    ppermute x13, starting transfers between devices, exchange(): return lax.ppermute(value, axis, [(i, i ^ mask) for i in range(count)])  29 us
    ppermute x13, waiting for transfers between devices, exchange(): return lax.ppermute(value, axis, [(i, i ^ mask) for i in range(count)])  6.23 us
    ppermute x4, starting transfers between devices, shifted(): lax.ppermute(value, 'row', [(i, (i + step) % count) for i in range(count)])  5.6 us
    pallas_call x1, Pallas kernels, gather_skeletons(): pl.pallas_call(gather_kernel, out_shape=(jax.ShapeDtypeStruct((64, 256),...  3.09 us
    pallas_call x3, Pallas kernels, near_product(): pl.pallas_call(functools.partial(near_kernel, offsets, len(parts), bool(e...  2.7 us
    dot_general x9, matrix products, times(): lax.dot_general(values, mats.astype(f32), (((1,), (0,)), ((), ())), preci...  2.11 us
    pallas_call x1, Pallas kernels, final_product(): pl.pallas_call(final_kernel, out_shape=jax.ShapeDtypeStruct((4, 512, 128)...  1.58 us
    dot_general x5, matrix products, times_t(): lax.dot_general(values, mats.astype(f32), (((1,), (1,)), ((), ())), preci...  1.41 us
  transfers between devices with their start and end apart: 17, of which 9 were waited for; matrix products, arithmetic and copies ran while one was open for 7% of the time, Pallas kernels for 7%

profile of v3, /device:TPU:1, one launch (start us, length us, event | category | flops | bytes accessed | tf_op | source)
XLA Modules:
  0.0 53.5 jit_solution(826002324818225043)
XLA Ops:
  0.0 3.1 %shard_map.91 = (f32[64,256]{1,0:T(8,128)S(1)}, f32[64,256]{1,0:T(8,128)S(1)}, f32[4,64,256]{2,1,0:T(8,128)S(1)}, bf16[4,64,256]{2,1,0:T(8,128)(2,1)S(1)}) custom-call(s32[1]{0:T(128)} %bitcast.half, bf16[4,512,128]{2,1,0:T(8,128)(2,1)} %refs_0_.1, bf16[4,512,256]{2,1,0:T(8,128)(2,1)} %basis.3, bf16[4,256,256]{2,1,0:T(8,128)(2,1)} %lt.5, bf16[2,256,256]{2,1,0:T(8,128)(2,1)} %mt.3), custom_call_target="tpu_custom_call" | custom-call | flops 134217728 | bytes 3145728 | tf_op jit(solution)/shard_map/pallas_call | solution.py:128
  3.1 2.1 %collective-permute-start = (f32[64,256]{1,0:T(8,128)S(1)}, f32[64,256]{1,0:T(8,128)S(1)}, u32[]{:S(2)}, u32[]{:S(2)}) collective-permute-start(f32[64,256]{1,0:T(8,128)S(1)} %get-tuple-element.31), channel_id=1, source_target_pairs={{0,1},{1,0},{2,3},{3,2},{4,5},{5,4},{6,7},{7,6},{8,9},{9,8},{10,11... | collective-permute-start | bytes 196616 | tf_op jit(solution)/shard_map/row_sum/ppermute | solution.py:18
  5.2 0.0 copy-done.5
  5.2 0.1 shard_map.92
  5.4 0.0 copy-start.2
  5.4 0.2 fusion.6
  5.6 0.3 fusion.7
  5.9 0.3 fusion.5
  6.1 0.8 %collective-permute-done = f32[64,256]{1,0:T(8,128)S(1)} collective-permute-done((f32[64,256]{1,0:T(8,128)S(1)}, f32[64,256]{1,0:T(8,128)S(1)}, u32[]{:S(2)}, u32[]{:S(2)}) %collective-permute-start) | collective-permute-done | bytes 65568 | tf_op jit(solution)/shard_map/row_sum/ppermute | solution.py:18
  6.9 2.8 %collective-permute-start.1 = (f32[64,256]{1,0:T(8,128)S(1)}, f32[64,256]{1,0:T(8,128)S(1)}, u32[]{:S(2)}, u32[]{:S(2)}) collective-permute-start(f32[64,256]{1,0:T(8,128)S(1)} %add.48.refs_0_), channel_id=1, source_target_pairs={{0,3},{1,2},{2,1},{3,0},{4,7},{5,6},{6,5},{7,4},{8,11},{9,10},{10,... | collective-permute-start | bytes 196616 | tf_op jit(solution)/shard_map/row_sum/ppermute | solution.py:18
  9.7 0.0 collective-permute-start.5
  9.7 1.5 %collective-permute-start.8 = (bf16[4,512,128]{2,1,0:T(8,128)(2,1)S(1)}, bf16[4,512,128]{2,1,0:T(8,128)(2,1)S(1)}, u32[]{:S(2)}, u32[]{:S(2)}) collective-permute-start(bf16[4,512,128]{2,1,0:T(8,128)(2,1)S(1)} %copy-done.2), channel_id=1, source_target_pairs={{0,1},{1,2},{2,3},{3,0},{4,5},{5,6},{6,7},{7,4},{8,9},{9,10},{10,1... | collective-permute-start | bytes 1572872 | tf_op jit(solution)/shard_map/row_sum/ring0/ppermute | solution.py:23
  11.2 0.2 collective-permute-done.1
  11.4 0.3 fusion.4
  11.7 5.8 %collective-permute-start.2 = (f32[96,256]{1,0:T(8,128)S(1)}, f32[96,256]{1,0:T(8,128)S(1)}, u32[]{:S(2)}, u32[]{:S(2)}) collective-permute-start(f32[96,256]{1,0:T(8,128)S(1)} %pad_maximum_fusion.refs_0_), channel_id=1, source_target_pairs={{0,4},{4,0},{8,12},{12,8},{16,20},{20,16},{24,28},{28,24},{32,36},... | collective-permute-start | bytes 294920 | tf_op jit(solution)/shard_map/level0/ppermute | solution.py:18
  17.4 0.9 %collective-permute-done.2 = f32[96,256]{1,0:T(8,128)S(1)} collective-permute-done((f32[96,256]{1,0:T(8,128)S(1)}, f32[96,256]{1,0:T(8,128)S(1)}, u32[]{:S(2)}, u32[]{:S(2)}) %collective-permute-start.2) | collective-permute-done | bytes 98336 | tf_op jit(solution)/shard_map/level0/ppermute | solution.py:18
  18.4 0.2 fusion.3
  18.7 0.1 collective-permute-start.3
  18.8 0.0 collective-permute-done.5.refs_1_
  18.8 1.7 %collective-permute-start.6 = (bf16[4,64,256]{2,1,0:T(8,128)(2,1)S(1)}, bf16[4,64,256]{2,1,0:T(8,128)(2,1)S(1)}, u32[]{:S(2)}, u32[]{:S(2)}) collective-permute-start(bf16[4,64,256]{2,1,0:T(8,128)(2,1)S(1)} %get-tuple-element.55), channel_id=1, source_target_pairs={{0,3},{1,2},{2,1},{3,0},{4,7},{5,6},{6,5},{7,4},{8,11},{9,10},{10,... | collective-permute-start | bytes 393224 | tf_op jit(solution)/shard_map/level1/side2/ppermute | solution.py:18
  20.5 1.1 %collective-permute-start.10 = (bf16[4,512,128]{2,1,0:T(8,128)(2,1)S(1)}, bf16[4,512,128]{2,1,0:T(8,128)(2,1)S(1)}, u32[]{:S(2)}, u32[]{:S(2)}) collective-permute-start(bf16[4,512,128]{2,1,0:T(8,128)(2,1)S(1)} %copy-done.2), channel_id=1, source_target_pairs={{0,3},{1,0},{2,1},{3,2},{4,7},{5,4},{6,5},{7,6},{8,11},{9,8},{10,9... | collective-permute-start | bytes 1572872 | tf_op jit(solution)/shard_map/level1/ring1/ppermute | solution.py:23
  21.6 0.4 collective-permute-done.3
  22.0 0.2 fusion.2
  22.3 2.3 %collective-permute-start.4 = (bf16[32,768]{1,0:T(8,128)(2,1)S(1)}, bf16[32,768]{1,0:T(8,128)(2,1)S(1)}, u32[]{:S(2)}, u32[]{:S(2)}) collective-permute-start(bf16[32,768]{1,0:T(8,128)(2,1)S(1)} %pad_maximum_fusion.2.signal), channel_id=1, source_target_pairs={{0,16},{4,20},{8,24},{12,28},{16,0},{20,4},{24,8},{28,12},{32,48},... | collective-permute-start | bytes 147464 | tf_op jit(solution)/shard_map/level2/ppermute | solution.py:18
  24.6 0.0 slice-done.1
  24.6 0.7 %near.6.refs_2_ = f32[4,512,128]{2,1,0:T(8,128)S(1)} custom-call(s32[1]{0:T(128)} %bitcast.1.place, bf16[4,512,2048]{2,1,0:T(8,128)(2,1)S(1)} %bitcast.46, bf16[32,768]{1,0:T(8,128)(2,1)S(1)} %pad_maximum_fusion.2.signal, bf16[4,512,128]{2,1,0:T(8,128)(2,1)S(1)} %copy-done.2), custom_call_target="tpu_custom_call" | custom-call | flops 2147483648 | bytes 4096 | tf_op jit(solution)/shard_map/level2/near/pallas_call | solution.py:194
  25.3 1.2 %collective-permute-done.4 = bf16[32,768]{1,0:T(8,128)(2,1)S(1)} collective-permute-done((bf16[32,768]{1,0:T(8,128)(2,1)S(1)}, bf16[32,768]{1,0:T(8,128)(2,1)S(1)}, u32[]{:S(2)}, u32[]{:S(2)}) %collective-permute-start.4) | collective-permute-done | bytes 49184 | tf_op jit(solution)/shard_map/level2/ppermute | solution.py:18
  26.5 0.2 fusion.1
  26.8 0.0 copy-start
  26.8 0.0 copy-start.6
  26.8 0.0 copy-start.7
  26.8 4.4 %collective-permute-start.9 = (bf16[32,768]{1,0:T(8,128)(2,1)S(1)}, bf16[32,768]{1,0:T(8,128)(2,1)S(1)}, u32[]{:S(2)}, u32[]{:S(2)}) collective-permute-start(bf16[32,768]{1,0:T(8,128)(2,1)S(1)} %pad_maximum_fusion.3.refs_0_.signal), channel_id=1, source_target_pairs={{0,48},{4,52},{8,56},{12,60},{16,32},{20,36},{24,40},{28,44},{32,1... | collective-permute-start | bytes 147464 | tf_op jit(solution)/shard_map/level3/ppermute | solution.py:18
  31.3 0.0 collective-permute-done.6.refs_1_
  31.3 0.7 %side3.3 = (f32[4,64,256]{2,1,0:T(8,128)S(1)}, bf16[4,64,256]{2,1,0:T(8,128)(2,1)S(1)}) custom-call(bf16[32,768]{1,0:T(8,128)(2,1)S(1)} %pad_maximum_fusion.3.refs_0_.signal, f32[4,64,256]{2,1,0:T(8,128)S(1)} %get-tuple-element.56.own, bf16[4,64,256]{2,1,0:T(8,128)(2,1)S(1)} %side3.2.got, bf16[4,256,256]{2,1,0:T(8,128)(2,1)S(1)} %copy-done, ...), custom_call_target="tpu_custom_call" | custom-call | flops 16777216 | bytes 4096 | tf_op jit(solution)/shard_map/level3/side3/pallas_call | solution.py:227
  32.0 0.6 %collective-permute-start.7 = (bf16[4,64,256]{2,1,0:T(8,128)(2,1)S(1)}, bf16[4,64,256]{2,1,0:T(8,128)(2,1)S(1)}, u32[]{:S(2)}, u32[]{:S(2)}) collective-permute-start(bf16[4,64,256]{2,1,0:T(8,128)(2,1)S(1)} %get-tuple-element.37), channel_id=1, source_target_pairs={{0,1},{1,0},{2,3},{3,2},{4,5},{5,4},{6,7},{7,6},{8,9},{9,8},{10,11... | collective-permute-start | bytes 393224 | tf_op jit(solution)/shard_map/level3/side3/ppermute | solution.py:18
  32.6 0.2 collective-permute-done.9
  32.8 0.2 fusion
  33.1 0.0 collective-permute-done.8.refs_1_
  33.1 1.4 %collective-permute-start.11 = (bf16[32,512]{1,0:T(8,128)(2,1)S(1)}, bf16[32,512]{1,0:T(8,128)(2,1)S(1)}, u32[]{:S(2)}, u32[]{:S(2)}) collective-permute-start(bf16[32,512]{1,0:T(8,128)(2,1)S(1)} %pad_maximum_fusion.4.refs_0_), channel_id=1, source_target_pairs={{0,64},{4,68},{8,72},{12,76},{16,80},{20,84},{24,88},{28,92},{32,9... | collective-permute-start | bytes 98312 | tf_op jit(solution)/shard_map/level4/ppermute | solution.py:18
  34.5 0.8 %collective-permute-start.15 = (bf16[2,512,128]{2,1,0:T(8,128)(2,1)S(1)}, bf16[2,512,128]{2,1,0:T(8,128)(2,1)S(1)}, u32[]{:S(2)}, u32[]{:S(2)}) collective-permute-start(bf16[2,512,128]{2,1,0:T(8,128)(2,1)S(1)} %slice.195), channel_id=1, source_target_pairs={{0,1},{1,2},{2,3},{3,0},{4,5},{5,6},{6,7},{7,4},{8,9},{9,10},{10,1... | collective-permute-start | bytes 786440 | tf_op jit(solution)/shard_map/level4/across/ppermute | solution.py:23
  35.4 0.6 %collective-permute-done.11 = bf16[32,512]{1,0:T(8,128)(2,1)S(1)} collective-permute-done((bf16[32,512]{1,0:T(8,128)(2,1)S(1)}, bf16[32,512]{1,0:T(8,128)(2,1)S(1)}, u32[]{:S(2)}, u32[]{:S(2)}) %collective-permute-start.11) | collective-permute-done | bytes 32800 | tf_op jit(solution)/shard_map/level4/ppermute | solution.py:18
  36.0 0.2 convolution_convert_fusion.refs_0_
  36.2 0.0 collective-permute-done.10.refs_1_
  36.2 0.0 collective-permute-done.7.side_other
  36.2 2.8 %collective-permute-start.12 = (bf16[32,256]{1,0:T(8,128)(2,1)S(1)}, bf16[32,256]{1,0:T(8,128)(2,1)S(1)}, u32[]{:S(2)}, u32[]{:S(2)}) collective-permute-start(bf16[32,256]{1,0:T(8,128)(2,1)S(1)} %convolution_convert_fusion.refs_0_), channel_id=1, source_target_pairs={{0,192},{4,196},{8,200},{12,204},{16,208},{20,212},{24,216},{28,22... | collective-permute-start | bytes 49160 | tf_op jit(solution)/shard_map/level5/ppermute | solution.py:18
  39.1 0.3 convolution_add_fusion.4
  39.3 0.3 convolution_add_fusion.3
  39.6 0.3 convolution_add_fusion.2
  39.9 2.2 %collective-permute-start.16 = (bf16[2,512,128]{2,1,0:T(8,128)(2,1)S(1)}, bf16[2,512,128]{2,1,0:T(8,128)(2,1)S(1)}, u32[]{:S(2)}, u32[]{:S(2)}) collective-permute-start(bf16[2,512,128]{2,1,0:T(8,128)(2,1)S(1)} %slice.196), channel_id=1, source_target_pairs={{0,3},{1,0},{2,1},{3,2},{4,7},{5,4},{6,5},{7,6},{8,11},{9,8},{10,9... | collective-permute-start | bytes 786440 | tf_op jit(solution)/shard_map/level4/across/ppermute | solution.py:23
  42.1 0.0 collective-permute-done.12
  42.1 0.3 convolution_add_fusion.1.refs_0_
  42.5 4.9 %collective-permute-start.13 = (f32[32,256]{1,0:T(8,128)S(1)}, f32[32,256]{1,0:T(8,128)S(1)}, u32[]{:S(2)}, u32[]{:S(2)}) collective-permute-start(f32[32,256]{1,0:T(8,128)S(1)} %convolution_add_fusion.1.refs_0_), channel_id=1, source_target_pairs={{0,4},{4,0},{8,12},{12,8},{16,20},{20,16},{24,28},{28,24},{32,36},... | collective-permute-start | bytes 98312 | tf_op jit(solution)/shard_map/down/ppermute | solution.py:18
  47.4 0.9 %collective-permute-done.13 = f32[32,256]{1,0:T(8,128)S(1)} collective-permute-done((f32[32,256]{1,0:T(8,128)S(1)}, f32[32,256]{1,0:T(8,128)S(1)}, u32[]{:S(2)}, u32[]{:S(2)}) %collective-permute-start.13) | collective-permute-done | bytes 32800 | tf_op jit(solution)/shard_map/down/ppermute | solution.py:18
  48.3 0.3 convolution_add_fusion.signal.own
  48.6 0.1 collective-permute-start.14
  48.7 1.3 %near.8.refs_2_ = f32[4,512,128]{2,1,0:T(8,128)S(1)} custom-call(s32[1]{0:T(128)} %bitcast.1.place, bf16[4,512,2048]{2,1,0:T(8,128)(2,1)S(1)} %bitcast.46, f32[64,256]{1,0:T(8,128)S(1)} %convolution_add_fusion.signal.own, bf16[4,512,128]{2,1,0:T(8,128)(2,1)S(1)} %across.3.refs_0_, bf16[4,512,128]{2,1,0:T(8,128)(2,1)S(1)} %across.2.refs_1_, ...), custom_call_target="tpu_custom_call" | custom-call | flops 2147483648 | bytes 4096 | tf_op jit(solution)/shard_map/down/near/pallas_call | solution.py:194
  50.0 0.0 copy-start.1
  50.0 0.0 copy-start.3
  50.0 0.0 collective-permute-done.15.refs_0_
  50.0 0.0 collective-permute-done.16.refs_1_
  50.0 0.7 %near.10 = f32[4,512,128]{2,1,0:T(8,128)S(1)} custom-call(s32[1]{0:T(128)} %bitcast.1.place, bf16[4,512,2048]{2,1,0:T(8,128)(2,1)S(1)} %bitcast.46, f32[64,256]{1,0:T(8,128)S(1)} %convolution_add_fusion.signal.own, bf16[2,512,128]{2,1,0:T(8,128)(2,1)S(1)} %collective-permute-done.15.refs_0_, bf16[2,512,128]{2,1,0:T(8,128)(2,1)S(1)} %collective-permute-done.16.refs_1_, ...), custom_call_target="tpu_custom_call" | custom-call | flops 2147483648 | bytes 4096 | tf_op jit(solution)/shard_map/down/near/pallas_call | solution.py:194
  50.7 1.1 %collective-permute-done.14.other = f32[64,256]{1,0:T(8,128)S(1)} collective-permute-done((f32[64,256]{1,0:T(8,128)S(1)}, f32[64,256]{1,0:T(8,128)S(1)}, u32[]{:S(2)}, u32[]{:S(2)}) %collective-permute-start.14) | collective-permute-done | bytes 65568 | tf_op jit(solution)/shard_map/down/ppermute | solution.py:18
  51.8 0.0 copy-done.1
  51.8 1.6 %final.1 = bf16[4,512,128]{2,1,0:T(8,128)(2,1)} custom-call(s32[1]{0:T(128)} %bitcast.half, f32[64,256]{1,0:T(8,128)S(1)} %convolution_add_fusion.signal.own, f32[64,256]{1,0:T(8,128)S(1)} %collective-permute-done.14.other, f32[4,64,256]{2,1,0:T(8,128)S(1)} %down.1.side_own, bf16[4,64,256]{2,1,0:T(8,128)(2,1)S(1)} %collective-permute-done.7.side_other, ...), custom_call_target="tpu_custom_call" | custom-call | flops 134217728 | bytes 4194304 | tf_op jit(solution)/shard_map/final/pallas_call | solution.py:280
  (47 shorter events, 0.3 us)
Async XLA Ops:
  0.0 5.2 %copy-start.5 = (bf16[1,5,256,256]{3,2,1,0:T(8,128)(2,1)S(1)}, bf16[1,5,256,256]{3,2,1,0:T(8,128)(2,1)}, u32[]{:S(2)}) copy-start(bf16[1,5,256,256]{3,2,1,0:T(8,128)(2,1)} %ct.1) | copy-start | bytes 1966084
  0.0 5.2 %copy-start.4 = (bf16[1,6,256,256]{3,2,1,0:T(8,128)(2,1)S(1)}, bf16[1,6,256,256]{3,2,1,0:T(8,128)(2,1)}, u32[]{:S(2)}) copy-start(bf16[1,6,256,256]{3,2,1,0:T(8,128)(2,1)} %cc.1) | copy-start | bytes 2359300
  3.1 3.8 %collective-permute-start = (f32[64,256]{1,0:T(8,128)S(1)}, f32[64,256]{1,0:T(8,128)S(1)}, u32[]{:S(2)}, u32[]{:S(2)}) collective-permute-start(f32[64,256]{1,0:T(8,128)S(1)} %get-tuple-element.31), channel_id=1, source_target_pairs={{0,1},{1,0},{2,3},{3,2},{4,5},{5,4},{6,7},{7,6},{8,9},{9,8},{10,11... | collective-permute-start | bytes 196616 | tf_op jit(solution)/shard_map/row_sum/ppermute | solution.py:18
  5.4 4.3 %copy-start.2 = (bf16[4,512,128]{2,1,0:T(8,128)(2,1)S(1)}, bf16[4,512,128]{2,1,0:T(8,128)(2,1)}, u32[]{:S(2)}) copy-start(bf16[4,512,128]{2,1,0:T(8,128)(2,1)} %refs_0_.1) | copy-start | bytes 1572868
  6.9 4.5 %collective-permute-start.1 = (f32[64,256]{1,0:T(8,128)S(1)}, f32[64,256]{1,0:T(8,128)S(1)}, u32[]{:S(2)}, u32[]{:S(2)}) collective-permute-start(f32[64,256]{1,0:T(8,128)S(1)} %add.48.refs_0_), channel_id=1, source_target_pairs={{0,3},{1,2},{2,1},{3,0},{4,7},{5,6},{6,5},{7,4},{8,11},{9,10},{10,... | collective-permute-start | bytes 196616 | tf_op jit(solution)/shard_map/row_sum/ppermute | solution.py:18
  9.7 9.1 %collective-permute-start.5 = (bf16[4,64,256]{2,1,0:T(8,128)(2,1)S(1)}, bf16[4,64,256]{2,1,0:T(8,128)(2,1)S(1)}, u32[]{:S(2)}, u32[]{:S(2)}) collective-permute-start(bf16[4,64,256]{2,1,0:T(8,128)(2,1)S(1)} %row_sum.1), channel_id=1, source_target_pairs={{0,1},{1,0},{2,3},{3,2},{4,5},{5,4},{6,7},{7,6},{8,9},{9,8},{10,11... | collective-permute-start | bytes 393224 | tf_op jit(solution)/shard_map/row_sum/ppermute | solution.py:18
  9.7 23.4 %collective-permute-start.8 = (bf16[4,512,128]{2,1,0:T(8,128)(2,1)S(1)}, bf16[4,512,128]{2,1,0:T(8,128)(2,1)S(1)}, u32[]{:S(2)}, u32[]{:S(2)}) collective-permute-start(bf16[4,512,128]{2,1,0:T(8,128)(2,1)S(1)} %copy-done.2), channel_id=1, source_target_pairs={{0,1},{1,2},{2,3},{3,0},{4,5},{5,6},{6,7},{7,4},{8,9},{9,10},{10,1... | collective-permute-start | bytes 1572872 | tf_op jit(solution)/shard_map/row_sum/ring0/ppermute | solution.py:23
  11.7 6.7 %collective-permute-start.2 = (f32[96,256]{1,0:T(8,128)S(1)}, f32[96,256]{1,0:T(8,128)S(1)}, u32[]{:S(2)}, u32[]{:S(2)}) collective-permute-start(f32[96,256]{1,0:T(8,128)S(1)} %pad_maximum_fusion.refs_0_), channel_id=1, source_target_pairs={{0,4},{4,0},{8,12},{12,8},{16,20},{20,16},{24,28},{28,24},{32,36},... | collective-permute-start | bytes 294920 | tf_op jit(solution)/shard_map/level0/ppermute | solution.py:18
  17.4 7.1 %slice-start = ((s8[8388608]{0:T(1024)(128)(4,1)}), s8[4194304]{0:T(1024)(128)(4,1)S(1)}, s32[]{:S(2)}) async-start(s8[8388608]{0:T(1024)(128)(4,1)} %bitcast.45), calls=%async_computation | async-start | bytes 8388608
  17.4 7.1 %slice-start.1 = ((s8[8388608]{0:T(1024)(128)(4,1)}), s8[4194304]{0:T(1024)(128)(4,1)S(1)}, s32[]{:S(2)}) async-start(s8[8388608]{0:T(1024)(128)(4,1)} %bitcast.45), calls=%async_computation.1 | async-start | bytes 8388608
  18.7 3.3 %collective-permute-start.3 = (bf16[32,768]{1,0:T(8,128)(2,1)S(1)}, bf16[32,768]{1,0:T(8,128)(2,1)S(1)}, u32[]{:S(2)}, u32[]{:S(2)}) collective-permute-start(bf16[32,768]{1,0:T(8,128)(2,1)S(1)} %pad_maximum_fusion.1.refs_0_), channel_id=1, source_target_pairs={{0,8},{4,12},{8,0},{12,4},{16,24},{20,28},{24,16},{28,20},{32,40},... | collective-permute-start | bytes 147464 | tf_op jit(solution)/shard_map/level1/ppermute | solution.py:18
  18.8 12.4 %collective-permute-start.6 = (bf16[4,64,256]{2,1,0:T(8,128)(2,1)S(1)}, bf16[4,64,256]{2,1,0:T(8,128)(2,1)S(1)}, u32[]{:S(2)}, u32[]{:S(2)}) collective-permute-start(bf16[4,64,256]{2,1,0:T(8,128)(2,1)S(1)} %get-tuple-element.55), channel_id=1, source_target_pairs={{0,3},{1,2},{2,1},{3,0},{4,7},{5,6},{6,5},{7,4},{8,11},{9,10},{10,... | collective-permute-start | bytes 393224 | tf_op jit(solution)/shard_map/level1/side2/ppermute | solution.py:18
  20.5 15.7 %collective-permute-start.10 = (bf16[4,512,128]{2,1,0:T(8,128)(2,1)S(1)}, bf16[4,512,128]{2,1,0:T(8,128)(2,1)S(1)}, u32[]{:S(2)}, u32[]{:S(2)}) collective-permute-start(bf16[4,512,128]{2,1,0:T(8,128)(2,1)S(1)} %copy-done.2), channel_id=1, source_target_pairs={{0,3},{1,0},{2,1},{3,2},{4,7},{5,4},{6,5},{7,6},{8,11},{9,8},{10,9... | collective-permute-start | bytes 1572872 | tf_op jit(solution)/shard_map/level1/ring1/ppermute | solution.py:23
  22.3 4.2 %collective-permute-start.4 = (bf16[32,768]{1,0:T(8,128)(2,1)S(1)}, bf16[32,768]{1,0:T(8,128)(2,1)S(1)}, u32[]{:S(2)}, u32[]{:S(2)}) collective-permute-start(bf16[32,768]{1,0:T(8,128)(2,1)S(1)} %pad_maximum_fusion.2.signal), channel_id=1, source_target_pairs={{0,16},{4,20},{8,24},{12,28},{16,0},{20,4},{24,8},{28,12},{32,48},... | collective-permute-start | bytes 147464 | tf_op jit(solution)/shard_map/level2/ppermute | solution.py:18
  26.8 4.5 %copy-start = (bf16[4,256,256]{2,1,0:T(8,128)(2,1)S(1)}, bf16[4,256,256]{2,1,0:T(8,128)(2,1)}, u32[]{:S(2)}) copy-start(bf16[4,256,256]{2,1,0:T(8,128)(2,1)} %lt.5) | copy-start | bytes 1572868
  26.8 4.5 %copy-start.6 = (bf16[2,256,256]{2,1,0:T(8,128)(2,1)S(1)}, bf16[2,256,256]{2,1,0:T(8,128)(2,1)}, u32[]{:S(2)}) copy-start(bf16[2,256,256]{2,1,0:T(8,128)(2,1)} %lc.1) | copy-start | bytes 786436
  26.8 4.4 %copy-start.7 = (bf16[1,256,256]{2,1,0:T(8,128)(2,1)S(1)}, bf16[1,256,256]{2,1,0:T(8,128)(2,1)}, u32[]{:S(2)}) copy-start(bf16[1,256,256]{2,1,0:T(8,128)(2,1)} %mc.1) | copy-start | bytes 393220
  26.8 6.0 %collective-permute-start.9 = (bf16[32,768]{1,0:T(8,128)(2,1)S(1)}, bf16[32,768]{1,0:T(8,128)(2,1)S(1)}, u32[]{:S(2)}, u32[]{:S(2)}) collective-permute-start(bf16[32,768]{1,0:T(8,128)(2,1)S(1)} %pad_maximum_fusion.3.refs_0_.signal), channel_id=1, source_target_pairs={{0,48},{4,52},{8,56},{12,60},{16,32},{20,36},{24,40},{28,44},{32,1... | collective-permute-start | bytes 147464 | tf_op jit(solution)/shard_map/level3/ppermute | solution.py:18
  32.0 4.2 %collective-permute-start.7 = (bf16[4,64,256]{2,1,0:T(8,128)(2,1)S(1)}, bf16[4,64,256]{2,1,0:T(8,128)(2,1)S(1)}, u32[]{:S(2)}, u32[]{:S(2)}) collective-permute-start(bf16[4,64,256]{2,1,0:T(8,128)(2,1)S(1)} %get-tuple-element.37), channel_id=1, source_target_pairs={{0,1},{1,0},{2,3},{3,2},{4,5},{5,4},{6,7},{7,6},{8,9},{9,8},{10,11... | collective-permute-start | bytes 393224 | tf_op jit(solution)/shard_map/level3/side3/ppermute | solution.py:18
  33.1 2.9 %collective-permute-start.11 = (bf16[32,512]{1,0:T(8,128)(2,1)S(1)}, bf16[32,512]{1,0:T(8,128)(2,1)S(1)}, u32[]{:S(2)}, u32[]{:S(2)}) collective-permute-start(bf16[32,512]{1,0:T(8,128)(2,1)S(1)} %pad_maximum_fusion.4.refs_0_), channel_id=1, source_target_pairs={{0,64},{4,68},{8,72},{12,76},{16,80},{20,84},{24,88},{28,92},{32,9... | collective-permute-start | bytes 98312 | tf_op jit(solution)/shard_map/level4/ppermute | solution.py:18
  34.5 15.4 %collective-permute-start.15 = (bf16[2,512,128]{2,1,0:T(8,128)(2,1)S(1)}, bf16[2,512,128]{2,1,0:T(8,128)(2,1)S(1)}, u32[]{:S(2)}, u32[]{:S(2)}) collective-permute-start(bf16[2,512,128]{2,1,0:T(8,128)(2,1)S(1)} %slice.195), channel_id=1, source_target_pairs={{0,1},{1,2},{2,3},{3,0},{4,5},{5,6},{6,7},{7,4},{8,9},{9,10},{10,1... | collective-permute-start | bytes 786440 | tf_op jit(solution)/shard_map/level4/across/ppermute | solution.py:23
  36.2 5.9 %collective-permute-start.12 = (bf16[32,256]{1,0:T(8,128)(2,1)S(1)}, bf16[32,256]{1,0:T(8,128)(2,1)S(1)}, u32[]{:S(2)}, u32[]{:S(2)}) collective-permute-start(bf16[32,256]{1,0:T(8,128)(2,1)S(1)} %convolution_convert_fusion.refs_0_), channel_id=1, source_target_pairs={{0,192},{4,196},{8,200},{12,204},{16,208},{20,212},{24,216},{28,22... | collective-permute-start | bytes 49160 | tf_op jit(solution)/shard_map/level5/ppermute | solution.py:18
  39.9 10.1 %collective-permute-start.16 = (bf16[2,512,128]{2,1,0:T(8,128)(2,1)S(1)}, bf16[2,512,128]{2,1,0:T(8,128)(2,1)S(1)}, u32[]{:S(2)}, u32[]{:S(2)}) collective-permute-start(bf16[2,512,128]{2,1,0:T(8,128)(2,1)S(1)} %slice.196), channel_id=1, source_target_pairs={{0,3},{1,0},{2,1},{3,2},{4,7},{5,4},{6,5},{7,6},{8,11},{9,8},{10,9... | collective-permute-start | bytes 786440 | tf_op jit(solution)/shard_map/level4/across/ppermute | solution.py:23
  42.5 5.8 %collective-permute-start.13 = (f32[32,256]{1,0:T(8,128)S(1)}, f32[32,256]{1,0:T(8,128)S(1)}, u32[]{:S(2)}, u32[]{:S(2)}) collective-permute-start(f32[32,256]{1,0:T(8,128)S(1)} %convolution_add_fusion.1.refs_0_), channel_id=1, source_target_pairs={{0,4},{4,0},{8,12},{12,8},{16,20},{20,16},{24,28},{28,24},{32,36},... | collective-permute-start | bytes 98312 | tf_op jit(solution)/shard_map/down/ppermute | solution.py:18
  48.6 3.2 %collective-permute-start.14 = (f32[64,256]{1,0:T(8,128)S(1)}, f32[64,256]{1,0:T(8,128)S(1)}, u32[]{:S(2)}, u32[]{:S(2)}) collective-permute-start(f32[64,256]{1,0:T(8,128)S(1)} %convolution_add_fusion.signal.own), channel_id=1, source_target_pairs={{0,1},{1,0},{2,3},{3,2},{4,5},{5,4},{6,7},{7,6},{8,9},{9,8},{10,11... | collective-permute-start | bytes 196616 | tf_op jit(solution)/shard_map/down/ppermute | solution.py:18
  50.0 1.8 %copy-start.1 = (bf16[4,512,256]{2,1,0:T(8,128)(2,1)S(1)}, bf16[4,512,256]{2,1,0:T(8,128)(2,1)}, u32[]{:S(2)}) copy-start(bf16[4,512,256]{2,1,0:T(8,128)(2,1)} %basis.3) | copy-start | bytes 3145732
  50.0 1.8 %copy-start.3 = (bf16[2,256,256]{2,1,0:T(8,128)(2,1)S(1)}, bf16[2,256,256]{2,1,0:T(8,128)(2,1)}, u32[]{:S(2)}) copy-start(bf16[2,256,256]{2,1,0:T(8,128)(2,1)} %mt.3) | copy-start | bytes 786436

commit v4 on v2

--- a/solution.py
+++ b/solution.py
@@ -262,18 +262,16 @@
     for n in range(4):
         side[n, mine, :] = side_own[n]
         side[n, rest, :] = side_other[n].astype(f32)
+    mids = [split_dot(pot[...], mt[pair], 1) for pair in range(2)]
+    lows = [(split_dot(mids[n // 2], lt[n], 1) + side[n]).astype(bf16) for n in range(4)]
     copies = []
-    for pair in range(2):
-        mid = split_dot(pot[...], mt[pair], 1)
-        for k in range(2):
-            n = 2 * pair + k
-            low = (split_dot(mid, lt[n], 1) + side[n]).astype(bf16)
-            far = lax.dot_general(
-                basis[n], low, (((1,), (1,)), ((), ())), preferred_element_type=f32
-            )
-            buf[n] = (near[n] + far).astype(bf16)
-            copies.append(pltpu.make_async_copy(buf.at[n], out.at[n], sems.at[n]))
-            copies[n].start()
+    for n in range(4):
+        far = lax.dot_general(
+            basis[n], lows[n], (((1,), (1,)), ((), ())), preferred_element_type=f32
+        )
+        buf[n] = (near[n] + far).astype(bf16)
+        copies.append(pltpu.make_async_copy(buf.at[n], out.at[n], sems.at[n]))
+        copies[n].start()
     for copy in copies:
         copy.wait()
 
@@ -347,7 +345,7 @@
     def prepare(level, current):
         both = times(current, joint[level])
         lifted = both[:, :256]
-        terms = two_terms(lifted)
+        terms = two_terms(lifted)[: 1 if level in (4,) else 2]
         payload = jnp.concatenate([*terms, both[:, 256:].astype(bf16)], axis=1)
         return lifted, payload
 

time: 53.3 us -> 53 us (level)
  no operation moved by 1% of the time
where the time goes in v4:
time: 53 us; the launch traced here: 52.8 us
  starting transfers between devices  34.6 us (65%)
  Pallas kernels  7.55 us (14%)
  waiting for transfers between devices  6.24 us (12%)
  matrix products  3.52 us (7%)
  between operations  0.58 us (1%)
    ppermute x13, starting transfers between devices, exchange(): return lax.ppermute(value, axis, [(i, i ^ mask) for i in range(count)])  29 us
    ppermute x13, waiting for transfers between devices, exchange(): return lax.ppermute(value, axis, [(i, i ^ mask) for i in range(count)])  6.23 us
    ppermute x4, starting transfers between devices, shifted(): lax.ppermute(value, 'row', [(i, (i + step) % count) for i in range(count)])  5.58 us
    pallas_call x3, Pallas kernels, near_product(): pl.pallas_call(functools.partial(near_kernel, offsets, len(parts), bool(e...  2.7 us
    pallas_call x1, Pallas kernels, gather_skeletons(): pl.pallas_call(gather_kernel, out_shape=(jax.ShapeDtypeStruct((64, 256),...  2.42 us
    dot_general x9, matrix products, times(): lax.dot_general(values, mats.astype(f32), (((1,), (0,)), ((), ())), preci...  2.11 us
    pallas_call x1, Pallas kernels, final_product(): pl.pallas_call(final_kernel, out_shape=jax.ShapeDtypeStruct((4, 512, 128)...  1.58 us
    dot_general x5, matrix products, times_t(): lax.dot_general(values, mats.astype(f32), (((1,), (1,)), ((), ())), preci...  1.41 us
  transfers between devices with their start and end apart: 17, of which 9 were waited for; matrix products, arithmetic and copies ran while one was open for 7% of the time, Pallas kernels for 7%

profile of v4, /device:TPU:1, one launch (start us, length us, event | category | flops | bytes accessed | tf_op | source)
XLA Modules:
  0.0 52.8 jit_solution(8834075097370967846)
XLA Ops:
  0.0 2.4 %shard_map.91 = (f32[64,256]{1,0:T(8,128)S(1)}, f32[64,256]{1,0:T(8,128)S(1)}, f32[4,64,256]{2,1,0:T(8,128)S(1)}, bf16[4,64,256]{2,1,0:T(8,128)(2,1)S(1)}) custom-call(s32[1]{0:T(128)} %bitcast.half, bf16[4,512,128]{2,1,0:T(8,128)(2,1)} %refs_0_.1, bf16[4,512,256]{2,1,0:T(8,128)(2,1)} %basis.3, bf16[4,256,256]{2,1,0:T(8,128)(2,1)} %lt.5, bf16[2,256,256]{2,1,0:T(8,128)(2,1)} %mt.3), custom_call_target="tpu_custom_call" | custom-call | flops 134217728 | bytes 3145728 | tf_op jit(solution)/shard_map/pallas_call | solution.py:129
  2.4 2.1 %collective-permute-start = (f32[64,256]{1,0:T(8,128)S(1)}, f32[64,256]{1,0:T(8,128)S(1)}, u32[]{:S(2)}, u32[]{:S(2)}) collective-permute-start(f32[64,256]{1,0:T(8,128)S(1)} %get-tuple-element.31), channel_id=1, source_target_pairs={{0,1},{1,0},{2,3},{3,2},{4,5},{5,4},{6,7},{7,6},{8,9},{9,8},{10,11... | collective-permute-start | bytes 196616 | tf_op jit(solution)/shard_map/row_sum/ppermute | solution.py:18
  4.6 0.1 shard_map.92
  4.7 0.0 copy-start.2
  4.7 0.2 fusion.6
  4.9 0.3 fusion.7
  5.2 0.3 fusion.5
  5.5 0.8 %collective-permute-done = f32[64,256]{1,0:T(8,128)S(1)} collective-permute-done((f32[64,256]{1,0:T(8,128)S(1)}, f32[64,256]{1,0:T(8,128)S(1)}, u32[]{:S(2)}, u32[]{:S(2)}) %collective-permute-start) | collective-permute-done | bytes 65568 | tf_op jit(solution)/shard_map/row_sum/ppermute | solution.py:18
  6.2 2.8 %collective-permute-start.1 = (f32[64,256]{1,0:T(8,128)S(1)}, f32[64,256]{1,0:T(8,128)S(1)}, u32[]{:S(2)}, u32[]{:S(2)}) collective-permute-start(f32[64,256]{1,0:T(8,128)S(1)} %add.48.refs_0_), channel_id=1, source_target_pairs={{0,3},{1,2},{2,1},{3,0},{4,7},{5,6},{6,5},{7,4},{8,11},{9,10},{10,... | collective-permute-start | bytes 196616 | tf_op jit(solution)/shard_map/row_sum/ppermute | solution.py:18
  9.1 0.0 collective-permute-start.5
  9.1 1.5 %collective-permute-start.8 = (bf16[4,512,128]{2,1,0:T(8,128)(2,1)S(1)}, bf16[4,512,128]{2,1,0:T(8,128)(2,1)S(1)}, u32[]{:S(2)}, u32[]{:S(2)}) collective-permute-start(bf16[4,512,128]{2,1,0:T(8,128)(2,1)S(1)} %copy-done.2), channel_id=1, source_target_pairs={{0,1},{1,2},{2,3},{3,0},{4,5},{5,6},{6,7},{7,4},{8,9},{9,10},{10,1... | collective-permute-start | bytes 1572872 | tf_op jit(solution)/shard_map/row_sum/ring0/ppermute | solution.py:23
  10.5 0.2 collective-permute-done.1
  10.7 0.3 fusion.4
  11.0 5.7 %collective-permute-start.2 = (f32[96,256]{1,0:T(8,128)S(1)}, f32[96,256]{1,0:T(8,128)S(1)}, u32[]{:S(2)}, u32[]{:S(2)}) collective-permute-start(f32[96,256]{1,0:T(8,128)S(1)} %pad_maximum_fusion.refs_0_), channel_id=1, source_target_pairs={{0,4},{4,0},{8,12},{12,8},{16,20},{20,16},{24,28},{28,24},{32,36},... | collective-permute-start | bytes 294920 | tf_op jit(solution)/shard_map/level0/ppermute | solution.py:18
  16.8 0.9 %collective-permute-done.2 = f32[96,256]{1,0:T(8,128)S(1)} collective-permute-done((f32[96,256]{1,0:T(8,128)S(1)}, f32[96,256]{1,0:T(8,128)S(1)}, u32[]{:S(2)}, u32[]{:S(2)}) %collective-permute-start.2) | collective-permute-done | bytes 98336 | tf_op jit(solution)/shard_map/level0/ppermute | solution.py:18
  17.7 0.2 fusion.3
  18.0 0.1 collective-permute-start.3
  18.1 0.0 collective-permute-done.5.refs_1_
  18.2 1.7 %collective-permute-start.6 = (bf16[4,64,256]{2,1,0:T(8,128)(2,1)S(1)}, bf16[4,64,256]{2,1,0:T(8,128)(2,1)S(1)}, u32[]{:S(2)}, u32[]{:S(2)}) collective-permute-start(bf16[4,64,256]{2,1,0:T(8,128)(2,1)S(1)} %get-tuple-element.55), channel_id=1, source_target_pairs={{0,3},{1,2},{2,1},{3,0},{4,7},{5,6},{6,5},{7,4},{8,11},{9,10},{10,... | collective-permute-start | bytes 393224 | tf_op jit(solution)/shard_map/level1/side2/ppermute | solution.py:18
  19.8 1.1 %collective-permute-start.10 = (bf16[4,512,128]{2,1,0:T(8,128)(2,1)S(1)}, bf16[4,512,128]{2,1,0:T(8,128)(2,1)S(1)}, u32[]{:S(2)}, u32[]{:S(2)}) collective-permute-start(bf16[4,512,128]{2,1,0:T(8,128)(2,1)S(1)} %copy-done.2), channel_id=1, source_target_pairs={{0,3},{1,0},{2,1},{3,2},{4,7},{5,4},{6,5},{7,6},{8,11},{9,8},{10,9... | collective-permute-start | bytes 1572872 | tf_op jit(solution)/shard_map/level1/ring1/ppermute | solution.py:23
  20.9 0.4 collective-permute-done.3
  21.3 0.2 fusion.2
  21.6 2.3 %collective-permute-start.4 = (bf16[32,768]{1,0:T(8,128)(2,1)S(1)}, bf16[32,768]{1,0:T(8,128)(2,1)S(1)}, u32[]{:S(2)}, u32[]{:S(2)}) collective-permute-start(bf16[32,768]{1,0:T(8,128)(2,1)S(1)} %pad_maximum_fusion.2.signal), channel_id=1, source_target_pairs={{0,16},{4,20},{8,24},{12,28},{16,0},{20,4},{24,8},{28,12},{32,48},... | collective-permute-start | bytes 147464 | tf_op jit(solution)/shard_map/level2/ppermute | solution.py:18
  23.9 0.0 slice-done.1
  23.9 0.7 %near.6.refs_2_ = f32[4,512,128]{2,1,0:T(8,128)S(1)} custom-call(s32[1]{0:T(128)} %bitcast.1.place, bf16[4,512,2048]{2,1,0:T(8,128)(2,1)S(1)} %bitcast.46, bf16[32,768]{1,0:T(8,128)(2,1)S(1)} %pad_maximum_fusion.2.signal, bf16[4,512,128]{2,1,0:T(8,128)(2,1)S(1)} %copy-done.2), custom_call_target="tpu_custom_call" | custom-call | flops 2147483648 | bytes 4096 | tf_op jit(solution)/shard_map/level2/near/pallas_call | solution.py:195
  24.6 1.2 %collective-permute-done.4 = bf16[32,768]{1,0:T(8,128)(2,1)S(1)} collective-permute-done((bf16[32,768]{1,0:T(8,128)(2,1)S(1)}, bf16[32,768]{1,0:T(8,128)(2,1)S(1)}, u32[]{:S(2)}, u32[]{:S(2)}) %collective-permute-start.4) | collective-permute-done | bytes 49184 | tf_op jit(solution)/shard_map/level2/ppermute | solution.py:18
  25.9 0.2 fusion.1
  26.1 0.0 copy-start
  26.2 0.0 copy-start.6
  26.2 0.0 copy-start.7
  26.2 4.4 %collective-permute-start.9 = (bf16[32,768]{1,0:T(8,128)(2,1)S(1)}, bf16[32,768]{1,0:T(8,128)(2,1)S(1)}, u32[]{:S(2)}, u32[]{:S(2)}) collective-permute-start(bf16[32,768]{1,0:T(8,128)(2,1)S(1)} %pad_maximum_fusion.3.refs_0_.signal), channel_id=1, source_target_pairs={{0,48},{4,52},{8,56},{12,60},{16,32},{20,36},{24,40},{28,44},{32,1... | collective-permute-start | bytes 147464 | tf_op jit(solution)/shard_map/level3/ppermute | solution.py:18
  30.6 0.0 collective-permute-done.6.refs_1_
  30.6 0.0 copy-done.6
  30.6 0.7 %side3.3 = (f32[4,64,256]{2,1,0:T(8,128)S(1)}, bf16[4,64,256]{2,1,0:T(8,128)(2,1)S(1)}) custom-call(bf16[32,768]{1,0:T(8,128)(2,1)S(1)} %pad_maximum_fusion.3.refs_0_.signal, f32[4,64,256]{2,1,0:T(8,128)S(1)} %get-tuple-element.56.own, bf16[4,64,256]{2,1,0:T(8,128)(2,1)S(1)} %side3.2.got, bf16[4,256,256]{2,1,0:T(8,128)(2,1)S(1)} %copy-done, ...), custom_call_target="tpu_custom_call" | custom-call | flops 16777216 | bytes 4096 | tf_op jit(solution)/shard_map/level3/side3/pallas_call | solution.py:228
  31.3 0.6 %collective-permute-start.7 = (bf16[4,64,256]{2,1,0:T(8,128)(2,1)S(1)}, bf16[4,64,256]{2,1,0:T(8,128)(2,1)S(1)}, u32[]{:S(2)}, u32[]{:S(2)}) collective-permute-start(bf16[4,64,256]{2,1,0:T(8,128)(2,1)S(1)} %get-tuple-element.37), channel_id=1, source_target_pairs={{0,1},{1,0},{2,3},{3,2},{4,5},{5,4},{6,7},{7,6},{8,9},{9,8},{10,11... | collective-permute-start | bytes 393224 | tf_op jit(solution)/shard_map/level3/side3/ppermute | solution.py:18
  32.0 0.2 collective-permute-done.9
  32.2 0.2 fusion
  32.5 0.0 collective-permute-done.8.refs_1_
  32.5 1.4 %collective-permute-start.11 = (bf16[32,512]{1,0:T(8,128)(2,1)S(1)}, bf16[32,512]{1,0:T(8,128)(2,1)S(1)}, u32[]{:S(2)}, u32[]{:S(2)}) collective-permute-start(bf16[32,512]{1,0:T(8,128)(2,1)S(1)} %pad_maximum_fusion.4.refs_0_), channel_id=1, source_target_pairs={{0,64},{4,68},{8,72},{12,76},{16,80},{20,84},{24,88},{28,92},{32,9... | collective-permute-start | bytes 98312 | tf_op jit(solution)/shard_map/level4/ppermute | solution.py:18
  33.9 0.8 %collective-permute-start.15 = (bf16[2,512,128]{2,1,0:T(8,128)(2,1)S(1)}, bf16[2,512,128]{2,1,0:T(8,128)(2,1)S(1)}, u32[]{:S(2)}, u32[]{:S(2)}) collective-permute-start(bf16[2,512,128]{2,1,0:T(8,128)(2,1)S(1)} %slice.195), channel_id=1, source_target_pairs={{0,1},{1,2},{2,3},{3,0},{4,5},{5,6},{6,7},{7,4},{8,9},{9,10},{10,1... | collective-permute-start | bytes 786440 | tf_op jit(solution)/shard_map/level4/across/ppermute | solution.py:23
  34.7 0.6 %collective-permute-done.11 = bf16[32,512]{1,0:T(8,128)(2,1)S(1)} collective-permute-done((bf16[32,512]{1,0:T(8,128)(2,1)S(1)}, bf16[32,512]{1,0:T(8,128)(2,1)S(1)}, u32[]{:S(2)}, u32[]{:S(2)}) %collective-permute-start.11) | collective-permute-done | bytes 32800 | tf_op jit(solution)/shard_map/level4/ppermute | solution.py:18
  35.3 0.2 convolution_convert_fusion.refs_0_
  35.5 0.0 collective-permute-done.10.refs_1_
  35.6 0.0 collective-permute-done.7.side_other
  35.6 2.8 %collective-permute-start.12 = (bf16[32,256]{1,0:T(8,128)(2,1)S(1)}, bf16[32,256]{1,0:T(8,128)(2,1)S(1)}, u32[]{:S(2)}, u32[]{:S(2)}) collective-permute-start(bf16[32,256]{1,0:T(8,128)(2,1)S(1)} %convolution_convert_fusion.refs_0_), channel_id=1, source_target_pairs={{0,192},{4,196},{8,200},{12,204},{16,208},{20,212},{24,216},{28,22... | collective-permute-start | bytes 49160 | tf_op jit(solution)/shard_map/level5/ppermute | solution.py:18
  38.4 0.3 convolution_add_fusion.4
  38.7 0.3 convolution_add_fusion.3
  38.9 0.3 convolution_add_fusion.2
  39.2 2.2 %collective-permute-start.16 = (bf16[2,512,128]{2,1,0:T(8,128)(2,1)S(1)}, bf16[2,512,128]{2,1,0:T(8,128)(2,1)S(1)}, u32[]{:S(2)}, u32[]{:S(2)}) collective-permute-start(bf16[2,512,128]{2,1,0:T(8,128)(2,1)S(1)} %slice.196), channel_id=1, source_target_pairs={{0,3},{1,0},{2,1},{3,2},{4,7},{5,4},{6,5},{7,6},{8,11},{9,8},{10,9... | collective-permute-start | bytes 786440 | tf_op jit(solution)/shard_map/level4/across/ppermute | solution.py:23
  41.5 0.0 collective-permute-done.12
  41.5 0.3 convolution_add_fusion.1.refs_0_
  41.8 4.9 %collective-permute-start.13 = (f32[32,256]{1,0:T(8,128)S(1)}, f32[32,256]{1,0:T(8,128)S(1)}, u32[]{:S(2)}, u32[]{:S(2)}) collective-permute-start(f32[32,256]{1,0:T(8,128)S(1)} %convolution_add_fusion.1.refs_0_), channel_id=1, source_target_pairs={{0,4},{4,0},{8,12},{12,8},{16,20},{20,16},{24,28},{28,24},{32,36},... | collective-permute-start | bytes 98312 | tf_op jit(solution)/shard_map/down/ppermute | solution.py:18
  46.7 0.9 %collective-permute-done.13 = f32[32,256]{1,0:T(8,128)S(1)} collective-permute-done((f32[32,256]{1,0:T(8,128)S(1)}, f32[32,256]{1,0:T(8,128)S(1)}, u32[]{:S(2)}, u32[]{:S(2)}) %collective-permute-start.13) | collective-permute-done | bytes 32800 | tf_op jit(solution)/shard_map/down/ppermute | solution.py:18
  47.6 0.3 convolution_add_fusion.signal.own
  47.9 0.1 collective-permute-start.14
  48.0 1.3 %near.8.refs_2_ = f32[4,512,128]{2,1,0:T(8,128)S(1)} custom-call(s32[1]{0:T(128)} %bitcast.1.place, bf16[4,512,2048]{2,1,0:T(8,128)(2,1)S(1)} %bitcast.46, f32[64,256]{1,0:T(8,128)S(1)} %convolution_add_fusion.signal.own, bf16[4,512,128]{2,1,0:T(8,128)(2,1)S(1)} %across.3.refs_0_, bf16[4,512,128]{2,1,0:T(8,128)(2,1)S(1)} %across.2.refs_1_, ...), custom_call_target="tpu_custom_call" | custom-call | flops 2147483648 | bytes 4096 | tf_op jit(solution)/shard_map/down/near/pallas_call | solution.py:195
  49.3 0.0 copy-start.1
  49.3 0.0 copy-start.3
  49.3 0.0 collective-permute-done.15.refs_0_
  49.3 0.0 collective-permute-done.16.refs_1_
  49.3 0.7 %near.10 = f32[4,512,128]{2,1,0:T(8,128)S(1)} custom-call(s32[1]{0:T(128)} %bitcast.1.place, bf16[4,512,2048]{2,1,0:T(8,128)(2,1)S(1)} %bitcast.46, f32[64,256]{1,0:T(8,128)S(1)} %convolution_add_fusion.signal.own, bf16[2,512,128]{2,1,0:T(8,128)(2,1)S(1)} %collective-permute-done.15.refs_0_, bf16[2,512,128]{2,1,0:T(8,128)(2,1)S(1)} %collective-permute-done.16.refs_1_, ...), custom_call_target="tpu_custom_call" | custom-call | flops 2147483648 | bytes 4096 | tf_op jit(solution)/shard_map/down/near/pallas_call | solution.py:195
  50.0 1.1 %collective-permute-done.14.other = f32[64,256]{1,0:T(8,128)S(1)} collective-permute-done((f32[64,256]{1,0:T(8,128)S(1)}, f32[64,256]{1,0:T(8,128)S(1)}, u32[]{:S(2)}, u32[]{:S(2)}) %collective-permute-start.14) | collective-permute-done | bytes 65568 | tf_op jit(solution)/shard_map/down/ppermute | solution.py:18
  51.1 0.0 copy-done.3
  51.1 1.6 %final.1 = bf16[4,512,128]{2,1,0:T(8,128)(2,1)} custom-call(s32[1]{0:T(128)} %bitcast.half, f32[64,256]{1,0:T(8,128)S(1)} %convolution_add_fusion.signal.own, f32[64,256]{1,0:T(8,128)S(1)} %collective-permute-done.14.other, f32[4,64,256]{2,1,0:T(8,128)S(1)} %down.1.side_own, bf16[4,64,256]{2,1,0:T(8,128)(2,1)S(1)} %collective-permute-done.7.side_other, ...), custom_call_target="tpu_custom_call" | custom-call | flops 134217728 | bytes 4194304 | tf_op jit(solution)/shard_map/final/pallas_call | solution.py:281
  (47 shorter events, 0.3 us)
Async XLA Ops:
  0.0 4.6 %copy-start.5 = (bf16[1,5,256,256]{3,2,1,0:T(8,128)(2,1)S(1)}, bf16[1,5,256,256]{3,2,1,0:T(8,128)(2,1)}, u32[]{:S(2)}) copy-start(bf16[1,5,256,256]{3,2,1,0:T(8,128)(2,1)} %ct.1) | copy-start | bytes 1966084
  0.0 4.6 %copy-start.4 = (bf16[1,6,256,256]{3,2,1,0:T(8,128)(2,1)S(1)}, bf16[1,6,256,256]{3,2,1,0:T(8,128)(2,1)}, u32[]{:S(2)}) copy-start(bf16[1,6,256,256]{3,2,1,0:T(8,128)(2,1)} %cc.1) | copy-start | bytes 2359300
  2.4 3.8 %collective-permute-start = (f32[64,256]{1,0:T(8,128)S(1)}, f32[64,256]{1,0:T(8,128)S(1)}, u32[]{:S(2)}, u32[]{:S(2)}) collective-permute-start(f32[64,256]{1,0:T(8,128)S(1)} %get-tuple-element.31), channel_id=1, source_target_pairs={{0,1},{1,0},{2,3},{3,2},{4,5},{5,4},{6,7},{7,6},{8,9},{9,8},{10,11... | collective-permute-start | bytes 196616 | tf_op jit(solution)/shard_map/row_sum/ppermute | solution.py:18
  4.7 4.3 %copy-start.2 = (bf16[4,512,128]{2,1,0:T(8,128)(2,1)S(1)}, bf16[4,512,128]{2,1,0:T(8,128)(2,1)}, u32[]{:S(2)}) copy-start(bf16[4,512,128]{2,1,0:T(8,128)(2,1)} %refs_0_.1) | copy-start | bytes 1572868
  6.2 4.5 %collective-permute-start.1 = (f32[64,256]{1,0:T(8,128)S(1)}, f32[64,256]{1,0:T(8,128)S(1)}, u32[]{:S(2)}, u32[]{:S(2)}) collective-permute-start(f32[64,256]{1,0:T(8,128)S(1)} %add.48.refs_0_), channel_id=1, source_target_pairs={{0,3},{1,2},{2,1},{3,0},{4,7},{5,6},{6,5},{7,4},{8,11},{9,10},{10,... | collective-permute-start | bytes 196616 | tf_op jit(solution)/shard_map/row_sum/ppermute | solution.py:18
  9.1 9.0 %collective-permute-start.5 = (bf16[4,64,256]{2,1,0:T(8,128)(2,1)S(1)}, bf16[4,64,256]{2,1,0:T(8,128)(2,1)S(1)}, u32[]{:S(2)}, u32[]{:S(2)}) collective-permute-start(bf16[4,64,256]{2,1,0:T(8,128)(2,1)S(1)} %row_sum.1), channel_id=1, source_target_pairs={{0,1},{1,0},{2,3},{3,2},{4,5},{5,4},{6,7},{7,6},{8,9},{9,8},{10,11... | collective-permute-start | bytes 393224 | tf_op jit(solution)/shard_map/row_sum/ppermute | solution.py:18
  9.1 23.4 %collective-permute-start.8 = (bf16[4,512,128]{2,1,0:T(8,128)(2,1)S(1)}, bf16[4,512,128]{2,1,0:T(8,128)(2,1)S(1)}, u32[]{:S(2)}, u32[]{:S(2)}) collective-permute-start(bf16[4,512,128]{2,1,0:T(8,128)(2,1)S(1)} %copy-done.2), channel_id=1, source_target_pairs={{0,1},{1,2},{2,3},{3,0},{4,5},{5,6},{6,7},{7,4},{8,9},{9,10},{10,1... | collective-permute-start | bytes 1572872 | tf_op jit(solution)/shard_map/row_sum/ring0/ppermute | solution.py:23
  11.0 6.7 %collective-permute-start.2 = (f32[96,256]{1,0:T(8,128)S(1)}, f32[96,256]{1,0:T(8,128)S(1)}, u32[]{:S(2)}, u32[]{:S(2)}) collective-permute-start(f32[96,256]{1,0:T(8,128)S(1)} %pad_maximum_fusion.refs_0_), channel_id=1, source_target_pairs={{0,4},{4,0},{8,12},{12,8},{16,20},{20,16},{24,28},{28,24},{32,36},... | collective-permute-start | bytes 294920 | tf_op jit(solution)/shard_map/level0/ppermute | solution.py:18
  16.8 7.1 %slice-start = ((s8[8388608]{0:T(1024)(128)(4,1)}), s8[4194304]{0:T(1024)(128)(4,1)S(1)}, s32[]{:S(2)}) async-start(s8[8388608]{0:T(1024)(128)(4,1)} %bitcast.45), calls=%async_computation | async-start | bytes 8388608
  16.8 7.1 %slice-start.1 = ((s8[8388608]{0:T(1024)(128)(4,1)}), s8[4194304]{0:T(1024)(128)(4,1)S(1)}, s32[]{:S(2)}) async-start(s8[8388608]{0:T(1024)(128)(4,1)} %bitcast.45), calls=%async_computation.1 | async-start | bytes 8388608
  18.0 3.3 %collective-permute-start.3 = (bf16[32,768]{1,0:T(8,128)(2,1)S(1)}, bf16[32,768]{1,0:T(8,128)(2,1)S(1)}, u32[]{:S(2)}, u32[]{:S(2)}) collective-permute-start(bf16[32,768]{1,0:T(8,128)(2,1)S(1)} %pad_maximum_fusion.1.refs_0_), channel_id=1, source_target_pairs={{0,8},{4,12},{8,0},{12,4},{16,24},{20,28},{24,16},{28,20},{32,40},... | collective-permute-start | bytes 147464 | tf_op jit(solution)/shard_map/level1/ppermute | solution.py:18
  18.2 12.4 %collective-permute-start.6 = (bf16[4,64,256]{2,1,0:T(8,128)(2,1)S(1)}, bf16[4,64,256]{2,1,0:T(8,128)(2,1)S(1)}, u32[]{:S(2)}, u32[]{:S(2)}) collective-permute-start(bf16[4,64,256]{2,1,0:T(8,128)(2,1)S(1)} %get-tuple-element.55), channel_id=1, source_target_pairs={{0,3},{1,2},{2,1},{3,0},{4,7},{5,6},{6,5},{7,4},{8,11},{9,10},{10,... | collective-permute-start | bytes 393224 | tf_op jit(solution)/shard_map/level1/side2/ppermute | solution.py:18
  19.8 15.7 %collective-permute-start.10 = (bf16[4,512,128]{2,1,0:T(8,128)(2,1)S(1)}, bf16[4,512,128]{2,1,0:T(8,128)(2,1)S(1)}, u32[]{:S(2)}, u32[]{:S(2)}) collective-permute-start(bf16[4,512,128]{2,1,0:T(8,128)(2,1)S(1)} %copy-done.2), channel_id=1, source_target_pairs={{0,3},{1,0},{2,1},{3,2},{4,7},{5,4},{6,5},{7,6},{8,11},{9,8},{10,9... | collective-permute-start | bytes 1572872 | tf_op jit(solution)/shard_map/level1/ring1/ppermute | solution.py:23
  21.6 4.2 %collective-permute-start.4 = (bf16[32,768]{1,0:T(8,128)(2,1)S(1)}, bf16[32,768]{1,0:T(8,128)(2,1)S(1)}, u32[]{:S(2)}, u32[]{:S(2)}) collective-permute-start(bf16[32,768]{1,0:T(8,128)(2,1)S(1)} %pad_maximum_fusion.2.signal), channel_id=1, source_target_pairs={{0,16},{4,20},{8,24},{12,28},{16,0},{20,4},{24,8},{28,12},{32,48},... | collective-permute-start | bytes 147464 | tf_op jit(solution)/shard_map/level2/ppermute | solution.py:18
  26.1 4.5 %copy-start = (bf16[4,256,256]{2,1,0:T(8,128)(2,1)S(1)}, bf16[4,256,256]{2,1,0:T(8,128)(2,1)}, u32[]{:S(2)}) copy-start(bf16[4,256,256]{2,1,0:T(8,128)(2,1)} %lt.5) | copy-start | bytes 1572868
  26.2 4.5 %copy-start.6 = (bf16[2,256,256]{2,1,0:T(8,128)(2,1)S(1)}, bf16[2,256,256]{2,1,0:T(8,128)(2,1)}, u32[]{:S(2)}) copy-start(bf16[2,256,256]{2,1,0:T(8,128)(2,1)} %lc.1) | copy-start | bytes 786436
  26.2 4.4 %copy-start.7 = (bf16[1,256,256]{2,1,0:T(8,128)(2,1)S(1)}, bf16[1,256,256]{2,1,0:T(8,128)(2,1)}, u32[]{:S(2)}) copy-start(bf16[1,256,256]{2,1,0:T(8,128)(2,1)} %mc.1) | copy-start | bytes 393220
  26.2 6.0 %collective-permute-start.9 = (bf16[32,768]{1,0:T(8,128)(2,1)S(1)}, bf16[32,768]{1,0:T(8,128)(2,1)S(1)}, u32[]{:S(2)}, u32[]{:S(2)}) collective-permute-start(bf16[32,768]{1,0:T(8,128)(2,1)S(1)} %pad_maximum_fusion.3.refs_0_.signal), channel_id=1, source_target_pairs={{0,48},{4,52},{8,56},{12,60},{16,32},{20,36},{24,40},{28,44},{32,1... | collective-permute-start | bytes 147464 | tf_op jit(solution)/shard_map/level3/ppermute | solution.py:18
  31.3 4.2 %collective-permute-start.7 = (bf16[4,64,256]{2,1,0:T(8,128)(2,1)S(1)}, bf16[4,64,256]{2,1,0:T(8,128)(2,1)S(1)}, u32[]{:S(2)}, u32[]{:S(2)}) collective-permute-start(bf16[4,64,256]{2,1,0:T(8,128)(2,1)S(1)} %get-tuple-element.37), channel_id=1, source_target_pairs={{0,1},{1,0},{2,3},{3,2},{4,5},{5,4},{6,7},{7,6},{8,9},{9,8},{10,11... | collective-permute-start | bytes 393224 | tf_op jit(solution)/shard_map/level3/side3/ppermute | solution.py:18
  32.5 2.9 %collective-permute-start.11 = (bf16[32,512]{1,0:T(8,128)(2,1)S(1)}, bf16[32,512]{1,0:T(8,128)(2,1)S(1)}, u32[]{:S(2)}, u32[]{:S(2)}) collective-permute-start(bf16[32,512]{1,0:T(8,128)(2,1)S(1)} %pad_maximum_fusion.4.refs_0_), channel_id=1, source_target_pairs={{0,64},{4,68},{8,72},{12,76},{16,80},{20,84},{24,88},{28,92},{32,9... | collective-permute-start | bytes 98312 | tf_op jit(solution)/shard_map/level4/ppermute | solution.py:18
  33.9 15.4 %collective-permute-start.15 = (bf16[2,512,128]{2,1,0:T(8,128)(2,1)S(1)}, bf16[2,512,128]{2,1,0:T(8,128)(2,1)S(1)}, u32[]{:S(2)}, u32[]{:S(2)}) collective-permute-start(bf16[2,512,128]{2,1,0:T(8,128)(2,1)S(1)} %slice.195), channel_id=1, source_target_pairs={{0,1},{1,2},{2,3},{3,0},{4,5},{5,6},{6,7},{7,4},{8,9},{9,10},{10,1... | collective-permute-start | bytes 786440 | tf_op jit(solution)/shard_map/level4/across/ppermute | solution.py:23
  35.6 5.9 %collective-permute-start.12 = (bf16[32,256]{1,0:T(8,128)(2,1)S(1)}, bf16[32,256]{1,0:T(8,128)(2,1)S(1)}, u32[]{:S(2)}, u32[]{:S(2)}) collective-permute-start(bf16[32,256]{1,0:T(8,128)(2,1)S(1)} %convolution_convert_fusion.refs_0_), channel_id=1, source_target_pairs={{0,192},{4,196},{8,200},{12,204},{16,208},{20,212},{24,216},{28,22... | collective-permute-start | bytes 49160 | tf_op jit(solution)/shard_map/level5/ppermute | solution.py:18
  39.2 10.1 %collective-permute-start.16 = (bf16[2,512,128]{2,1,0:T(8,128)(2,1)S(1)}, bf16[2,512,128]{2,1,0:T(8,128)(2,1)S(1)}, u32[]{:S(2)}, u32[]{:S(2)}) collective-permute-start(bf16[2,512,128]{2,1,0:T(8,128)(2,1)S(1)} %slice.196), channel_id=1, source_target_pairs={{0,3},{1,0},{2,1},{3,2},{4,7},{5,4},{6,5},{7,6},{8,11},{9,8},{10,9... | collective-permute-start | bytes 786440 | tf_op jit(solution)/shard_map/level4/across/ppermute | solution.py:23
  41.8 5.8 %collective-permute-start.13 = (f32[32,256]{1,0:T(8,128)S(1)}, f32[32,256]{1,0:T(8,128)S(1)}, u32[]{:S(2)}, u32[]{:S(2)}) collective-permute-start(f32[32,256]{1,0:T(8,128)S(1)} %convolution_add_fusion.1.refs_0_), channel_id=1, source_target_pairs={{0,4},{4,0},{8,12},{12,8},{16,20},{20,16},{24,28},{28,24},{32,36},... | collective-permute-start | bytes 98312 | tf_op jit(solution)/shard_map/down/ppermute | solution.py:18
  47.9 3.2 %collective-permute-start.14 = (f32[64,256]{1,0:T(8,128)S(1)}, f32[64,256]{1,0:T(8,128)S(1)}, u32[]{:S(2)}, u32[]{:S(2)}) collective-permute-start(f32[64,256]{1,0:T(8,128)S(1)} %convolution_add_fusion.signal.own), channel_id=1, source_target_pairs={{0,1},{1,0},{2,3},{3,2},{4,5},{5,4},{6,7},{7,6},{8,9},{9,8},{10,11... | collective-permute-start | bytes 196616 | tf_op jit(solution)/shard_map/down/ppermute | solution.py:18
  49.3 1.8 %copy-start.1 = (bf16[4,512,256]{2,1,0:T(8,128)(2,1)S(1)}, bf16[4,512,256]{2,1,0:T(8,128)(2,1)}, u32[]{:S(2)}) copy-start(bf16[4,512,256]{2,1,0:T(8,128)(2,1)} %basis.3) | copy-start | bytes 3145732
  49.3 1.8 %copy-start.3 = (bf16[2,256,256]{2,1,0:T(8,128)(2,1)S(1)}, bf16[2,256,256]{2,1,0:T(8,128)(2,1)}, u32[]{:S(2)}) copy-start(bf16[2,256,256]{2,1,0:T(8,128)(2,1)} %mt.3) | copy-start | bytes 786436
